TPU v7x, 32 devices: a whole 2x2x4 slice. The times are simulated.
32 devices in a mesh: section: 2 (over x), mp: 16 (over z, y, core).
Axes of the slice: x: 2, y: 2, z: 4, core: 2. Of those that a mesh axis runs over, the one named last changes fastest.
Arguments:
- enc_final: bfloat16 [2, 128, 4096], P('section', None, 'mp'), may hold values from -64 to 64
- enc_len: int32 [2], replicated, may hold values from 32 to 128, as said below
- kv_weight: bfloat16 [2, 4096, 2, 4096], P('section', None, None, 'mp'), may hold values from -1 to 1
- queries: bfloat16 [2, 2, 512, 4096], P('section', None, None, 'mp'), may hold values from -4096 to 4096
- d_context: bfloat16 [2, 2, 512, 4096], P('section', None, None, 'mp'), may hold values from -6 to 6
Outputs:
- context: bfloat16 [2, 2, 512, 4096], P('section', None, None, 'mp')
- query_grad: bfloat16 [2, 2, 512, 4096], P('section', None, None, 'mp')
- kv_weight_grad: bfloat16 [2, 4096, 2, 4096], P('section', None, None, 'mp')
- enc_grad: bfloat16 [2, 128, 4096], P('section', None, 'mp')
Inputs may be any that keep to these rules, and one draw needn't show every extreme that they name: `enc_len`: some microbatch has exactly 128 valid positions.
All inputs are finite; a program needn't handle non-finite values.
Results may differ from a plain program's by a relative error of at most 0.02.
Values may be sent and summed in bfloat16 or wider, within the bound.
A program may use at most 128 MiB of HBM per device.

v0:
```python
import jax
import jax.numpy as jnp
from jax import lax
from jax.sharding import PartitionSpec as P

HD = 64


def shards(enc_final, enc_len, kv_weight, queries, d_context):
    model_width = kv_weight.shape[1]
    local_cols = kv_weight.shape[3]
    heads_dev = local_cols // HD
    micro = queries.shape[1]
    targets = queries.shape[2]
    sources = enc_final.shape[1]
    across = lax.all_gather(enc_final, "section", axis=0, tiled=True)
    states = lax.all_gather(across, "mp", axis=2, tiled=True)
    states_flat = states.reshape(micro * sources, model_width)
    weight_flat = kv_weight.reshape(model_width, 2 * local_cols)
    key_value = jnp.dot(states_flat, weight_flat, preferred_element_type=jnp.float32).astype(
        jnp.bfloat16
    )
    key_value = key_value.reshape(micro, sources, 2, heads_dev, HD)
    key_heads = key_value[:, :, 0]
    value_heads = key_value[:, :, 1]
    query_heads = queries.reshape(micro, targets, heads_dev, HD)
    grad_heads = d_context.reshape(micro, targets, heads_dev, HD)
    factor = HD ** (-0.5)
    scores = (
        jnp.einsum("mthd,mshd->mhts", query_heads, key_heads, preferred_element_type=jnp.float32)
        * factor
    )
    position = jnp.arange(sources, dtype=jnp.int32)
    valid_key = position[None, :] < enc_len[:, None]
    scores = jnp.where(valid_key[:, None, None, :], scores, -1e30)
    row_peak = jnp.max(scores, axis=-1, keepdims=True)
    exponent = jnp.exp(scores - row_peak)
    attn_prob = exponent / jnp.sum(exponent, axis=-1, keepdims=True)
    rounded = attn_prob.astype(jnp.bfloat16)
    context = jnp.einsum(
        "mhts,mshd->mthd", rounded, value_heads, preferred_element_type=jnp.float32
    ).astype(jnp.bfloat16)
    value_grad = jnp.einsum(
        "mhts,mthd->mshd", rounded, grad_heads, preferred_element_type=jnp.float32
    )
    prob_grad = jnp.einsum(
        "mthd,mshd->mhts", grad_heads, value_heads, preferred_element_type=jnp.float32
    )
    score_grad = attn_prob * (prob_grad - jnp.sum(prob_grad * attn_prob, axis=-1, keepdims=True))
    score_rounded = (score_grad * factor).astype(jnp.bfloat16)
    key_grad = jnp.einsum(
        "mhts,mthd->mshd", score_rounded, query_heads, preferred_element_type=jnp.float32
    )
    query_grad = jnp.einsum(
        "mhts,mshd->mthd", score_rounded, key_heads, preferred_element_type=jnp.float32
    ).astype(jnp.bfloat16)
    kv_grad = (
        jnp.stack([key_grad, value_grad], axis=2)
        .astype(jnp.bfloat16)
        .reshape(micro * sources, 2 * local_cols)
    )
    weight_grad = lax.dot_general(
        states_flat, kv_grad, (((0,), (0,)), ((), ())), preferred_element_type=jnp.float32
    )
    weight_grad = weight_grad.astype(jnp.bfloat16).reshape(1, model_width, 2, local_cols)
    kv_blocks = kv_grad.reshape(micro, sources, 2 * local_cols)
    full_term = jnp.einsum(
        "msk,dk->msd", kv_blocks, weight_flat, preferred_element_type=jnp.float32
    )
    feature_sum = lax.psum_scatter(
        full_term.astype(jnp.bfloat16), "mp", scatter_dimension=2, tiled=True
    )
    enc_grad = lax.psum_scatter(feature_sum, "section", scatter_dimension=0, tiled=True).astype(
        jnp.float32
    )
    return (
        context.reshape(1, micro, targets, local_cols),
        query_grad.reshape(1, micro, targets, local_cols),
        weight_grad,
        enc_grad.astype(jnp.bfloat16),
    )


def solution(mesh):
    return jax.shard_map(
        shards,
        mesh=mesh,
        in_specs=(
            P("section", None, "mp"),
            P(),
            P("section", None, None, "mp"),
            P("section", None, None, "mp"),
            P("section", None, None, "mp"),
        ),
        out_specs=(
            P("section", None, None, "mp"),
            P("section", None, None, "mp"),
            P("section", None, None, "mp"),
            P("section", None, "mp"),
        ),
        check_vma=False,
    )
```

profile of v0, /device:TPU:0, one launch (start us, length us, event | category | flops | bytes accessed | tf_op | source)
XLA Modules:
  0.0 156.0 jit_solution(12280002718195157123)
XLA Ops:
  7.2 0.0 all-gather.2.cloned.1.call-start
  7.2 7.6 %all_gather.6 = bf16[2,128,256]{2,1,0:T(8,128)(2,1)} all-gather(bf16[1,128,256]{2,1,0:T(8,128)(2,1)} %param.5), channel_id=1, replica_groups=mesh['section'=2,'mp'=16] {'section'}, dimensions={0}, use_global_device_ids=true | all-gather | bytes 196608 | tf_op jit(solution)/shard_map/all_gather | solution.py:16
  14.8 0.0 all-gather.2.cloned.1.call-update
  14.8 0.0 reduce-scatter.3.cloned.1.call-start
  14.9 1.3 copy.40
  16.1 1.3 copy.42
  17.4 7.6 %reshape.77 = bf16[4096,512,1]{1,0,2:T(8,128)(2,1)} reshape(bf16[1,4096,2,256]{3,2,1,0:T(2,128)(2,1)} %param.7) | data formatting | bytes 8388608 | tf_op jit(solution)/shard_map/reshape | solution.py:19
  25.0 0.0 copy-start.2
  25.0 4.9 %copy.61 = bf16[512,8,2,256]{3,1,2,0:T(8,128)(2,1)} copy(bf16[512,8,2,256]{3,2,1,0:T(2,128)(2,1)} %bitcast.92) | data formatting | bytes 8388608
  30.0 0.0 copy-done.2
  30.0 0.1 iota_compare_fusion
  30.1 26.5 %all-gather.2.cloned.1.call-done = bf16[2,128,4096]{2,1,0:T(8,128)(2,1)} async-done(((bf16[2,128,256]{2,1,0:T(8,128)(2,1)}), bf16[2,128,4096]{2,1,0:T(8,128)(2,1)}) %all-gather.2.cloned.1.call-update) | async-done | bytes 2097168 | tf_op jit(solution)/shard_map/all_gather | solution.py:17
  56.5 4.1 %convolution_convert_fusion.4 = bf16[256,512]{1,0:T(8,128)(2,1)S(1)} fusion(bf16[256,4096]{1,0:T(8,128)(2,1)} %bitcast.95, bf16[4096,512]{1,0:T(8,128)(2,1)} %bitcast.94), kind=kOutput, calls=%fused_computation.16 | convolution fusion | flops 1073872896 | bytes 6553600 | tf_op jit(solution)/shard_map/dot_general | solution.py:20
  60.6 0.3 reshape.79
  60.9 0.2 fusion.38
  61.1 0.2 copy.60
  61.2 0.2 copy.59
  61.4 0.5 fusion.29
  61.9 0.0 copy-start.1
  61.9 2.2 %fusion.39 = (f32[2,4,512]{2,1,0:T(4,128)S(1)}, f32[2,4,512,128]{2,3,1,0:T(8,128)}) fusion(pred[2,128]{1,0:T(4,128)(4,1)S(1)} %iota_compare_fusion, bf16[2,512,4,64]{1,3,2,0:T(8,128)(2,1)S(1)} %bitcast.101, bf16[2,128,1,4,64]{1,4,3,0,2:T(8,128)(2,1)S(1)} %copy.60), kind=kOutput, calls=%fused_computation.47 | convolution fusion | flops 69206144 | bytes 2769152 | tf_op jit(solution)/shard_map/sub | solution.py:37
  64.1 2.1 %fusion.10 = bf16[2,128,1,4,64]{1,4,3,0,2:T(8,128)(2,1)S(1)} fusion(bf16[2,512,4,64]{1,3,2,0:T(8,128)(2,1)S(1)} %bitcast.98, f32[2,4,512,128]{2,3,1,0:T(8,128)} %get-tuple-element.19, f32[2,4,512]{2,1,0:T(4,128)S(1)} %get-tuple-element.18), kind=kOutput, calls=%fused_computation.20 | convolution fusion | flops 68222976 | bytes 2768896 | tf_op jit(solution)/shard_map/mhts,mthd->mshd/dot_general | solution.py:43
  66.2 0.0 copy-done.1
  66.2 3.1 %fusion.9 = bf16[2,128,1,4,64]{1,4,3,0,2:T(8,128)(2,1)S(1)} fusion(bf16[2,512,4,64]{1,3,2,0:T(8,128)(2,1)S(1)} %bitcast.102, f32[2,4,128,512]{3,2,1,0:T(8,128)S(1)} %fusion.29, f32[2,4,512,128]{2,3,1,0:T(8,128)} %get-tuple-element.19, f32[2,4,512]{2,1,0:T(4,128)S(1)} %get-tuple-element.18), kind=kOutput, calls=%fused_computation.19 | convolution fusion | flops 70848640 | bytes 4866048 | tf_op jit(solution)/shard_map/mhts,mthd->mshd/dot_general | solution.py:51
  69.4 4.9 %convolution_convert_fusion.1 = bf16[2,128,4096]{2,1,0:T(8,128)(2,1)} fusion(bf16[2,128,512]{1,2,0:T(8,128)(2,1)S(1)} %bitcast.100, bf16[4096,512,1]{1,0,2:T(8,128)(2,1)} %reshape.77), kind=kOutput, calls=%fused_computation.3 | convolution fusion | flops 1074790400 | bytes 6553600 | tf_op jit(solution)/shard_map/msk,dk->msd/dot_general | solution.py:67
  74.4 0.0 reduce-scatter.3.cloned.1.call-update
  74.4 0.0 reduce-scatter.5.cloned.1.call-start
  74.4 0.3 copy.46
  74.7 1.9 %convolution_convert_fusion.3 = bf16[2,4,64,512]{3,2,1,0:T(8,128)(2,1)S(1)} fusion(bf16[2,128,1,4,64]{1,4,3,0,2:T(8,128)(2,1)S(1)} %copy.59, f32[2,4,512,128]{2,3,1,0:T(8,128)} %get-tuple-element.19, f32[2,4,512]{2,1,0:T(4,128)S(1)} %get-tuple-element.18), kind=kOutput, calls=%fused_computation.15 | convolution fusion | flops 68419584 | bytes 2768896 | tf_op jit(solution)/shard_map/mhts,mshd->mthd/dot_general | solution.py:40
  76.6 1.0 copy.49
  77.6 0.0 copy-start
  77.6 4.6 %convolution_convert_fusion.2 = bf16[2,4,64,512]{3,2,1,0:T(8,128)(2,1)S(1)} fusion(f32[2,4,128,512]{3,2,1,0:T(8,128)} %copy-done.1, bf16[2,128,1,4,64]{1,4,3,0,2:T(8,128)(2,1)S(1)} %copy.60, f32[2,4,512,128]{2,3,1,0:T(8,128)} %get-tuple-element.19, f32[2,4,512]{2,1,0:T(4,128)S(1)} %get-tuple-element.18), kind=kOutput, calls=%fused_computation.14 | convolution fusion | flops 71045248 | bytes 4866048 | tf_op jit(solution)/shard_map/mhts,mshd->mthd/dot_general | solution.py:54
  82.3 1.0 copy.50
  83.3 51.8 %reduce-scatter.3.cloned.1.call-done = bf16[2,128,256]{2,1,0:T(8,128)(2,1)} async-done(((bf16[2,128,4096]{2,1,0:T(8,128)(2,1)}), bf16[2,128,256]{2,1,0:T(8,128)(2,1)}) %reduce-scatter.3.cloned.1.call-update) | async-done | bytes 131088 | tf_op jit(solution)/shard_map/reduce_scatter | solution.py:70
  135.0 0.0 reduce-scatter.5.cloned.1.call-update
  135.1 0.0 copy-done
  135.1 3.3 %convolution_convert_fusion = bf16[512,4096]{1,0:T(8,128)(2,1)} fusion(bf16[256,4096]{1,0:T(8,128)(2,1)S(1)} %bitcast.96, bf16[64,8,2,128]{3,2,1,0:T(2,128)(2,1)S(1)} %bitcast.99), kind=kOutput, calls=%fused_computation.2 | convolution fusion | flops 1075838976 | bytes 6553600 | tf_op jit(solution)/shard_map/dot_general | solution.py:62
  138.4 11.1 %copy.51 = bf16[1,4096,2,256]{3,2,1,0:T(2,128)(2,1)} copy(bf16[1,4096,2,256]{1,3,2,0:T(8,128)(2,1)} %bitcast.93) | data formatting | bytes 8388608
  149.5 0.0 reduce-scatter.5.cloned.1.call-done
  (2 shorter events, 0.0 us)
Async XLA Ops:
  7.2 49.4 %all-gather.2.cloned.1.call-start = ((), (), s32[]{:S(2)}) async-start(), calls=%async_computation.2 | async-start | bytes 2228224 | tf_op jit(solution)/shard_map/all_gather | solution.py:17
  14.8 120.2 %reduce-scatter.3.cloned.1.call-start = ((), (), s32[]{:S(2)}) async-start(), calls=%async_computation.3 | async-start | bytes 2228224 | tf_op jit(solution)/shard_map/reduce_scatter | solution.py:70
  25.0 4.9 %copy-start.2 = (s32[2]{0:T(128)S(1)}, s32[2]{0:T(128)}, u32[]{:S(2)}) copy-start(s32[2]{0:T(128)} %param.6) | copy-start | bytes 28
  61.9 4.3 %copy-start.1 = (f32[2,4,128,512]{3,2,1,0:T(8,128)}, f32[2,4,128,512]{3,2,1,0:T(8,128)S(1)}, u32[]{:S(2)}) copy-start(f32[2,4,128,512]{3,2,1,0:T(8,128)S(1)} %fusion.29) | copy-start | bytes 6291460
  74.4 75.1 %reduce-scatter.5.cloned.1.call-start = ((), (), s32[]{:S(2)}) async-start(), calls=%async_computation.4 | async-start | bytes 196608 | tf_op jit(solution)/shard_map/reduce_scatter | solution.py:73
  77.6 57.5 %copy-start = (bf16[2,128,4096]{2,1,0:T(8,128)(2,1)S(1)}, bf16[2,128,4096]{2,1,0:T(8,128)(2,1)}, u32[]{:S(2)}) copy-start(bf16[2,128,4096]{2,1,0:T(8,128)(2,1)} %all-gather.2.cloned.1.call-done) | copy-start | bytes 6291460
Sparse Core Ops, SparseCore 0:
  15.0 41.5 all-gather.1
  74.5 60.4 reduce-scatter.2
  137.9 9.2 reduce-scatter.4
where the time goes:
time: 157 us; the launch traced here: 156 us
  waiting for transfers between devices  78.3 us (50%)
  local copies, waits for them, and re-layouts  29.3 us (19%)
  matrix products  26.7 us (17%)
  between operations  13.9 us (9%)
  blocking collectives  7.6 us (5%)
    reduce_scatter x1, waiting for transfers between devices, shards(): lax.psum_scatter(full_term.astype(jnp.bfloat16), 'mp', scatter_dimension=...  51.8 us
    all_gather x1, waiting for transfers between devices, shards(): states = lax.all_gather(across, 'mp', axis=2, tiled=True)  26.5 us
    unnamed x14, local copies, waits for them, and re-layouts  20.9 us
    reshape x1, local copies, waits for them, and re-layouts, shards(): weight_flat = kv_weight.reshape(model_width, 2 * local_cols)  7.63 us
    all_gather x1, blocking collectives, shards(): across = lax.all_gather(enc_final, 'section', axis=0, tiled=True)  7.6 us
    dot_general x1, matrix products, shards(): jnp.einsum('msk,dk->msd', kv_blocks, weight_flat, preferred_element_type=...  4.94 us
    dot_general x1, matrix products, shards(): jnp.einsum('mhts,mshd->mthd', score_rounded, key_heads, preferred_element...  4.64 us
    dot_general x1, matrix products, shards(): jnp.dot(states_flat, weight_flat, preferred_element_type=jnp.float32)  4.06 us
  transfers between devices with their start and end apart: 3, of which 2 were waited for; matrix products, arithmetic and copies ran while one was open for 25% of the time, Pallas kernels for 0%

commit v1 on v0

v1 whole, which is shorter than its diff:
```python
import functools

import jax
import jax.numpy as jnp
from jax import lax
from jax.experimental import pallas as pl
from jax.experimental.pallas import tpu as pltpu
from jax.sharding import PartitionSpec as P

HD = 64
LANES = 128
MESH = pl.DeviceIdType.MESH
VMEM_BYTES = 56 * 2**20
NT = (((1,), (1,)), ((), ()))
TN = (((0,), (0,)), ((), ()))


def wrap(value, size):
    return lax.rem(value, size)


class Grid:
    def __init__(self, section, mp):
        self.S, self.M = section, mp
        self.C = 2 if mp % 2 == 0 else 1
        self.Y = 2 if (mp // self.C) % 2 == 0 else 1
        self.Z = mp // self.C // self.Y

    def here(self):
        x, p = lax.axis_index("section"), lax.axis_index("mp")
        c = lax.rem(p, self.C)
        zy = lax.div(p, self.C)
        return x, lax.div(zy, self.Y), lax.rem(zy, self.Y), c

    def p(self, z, y, c):
        return (z * self.Y + y) * self.C + c

    def tile(self, x, z, y, c):
        return x * self.M + self.p(z, y, c)

    def device(self, x, z, y, c):
        return (x, self.p(z, y, c))

    def barrier(self):
        x, z, y, c = self.here()
        sem = pltpu.get_barrier_semaphore()
        peers = [self.device(wrap(x + d, self.S), z, y, c) for d in range(1, self.S)]
        peers += [self.device(x, wrap(z + d, self.Z), y, c) for d in range(1, self.Z)]
        peers += [self.device(x, z, wrap(y + d, self.Y), c) for d in range(1, self.Y)]
        peers += [self.device(x, z, y, wrap(c + d, self.C)) for d in range(1, self.C)]
        for peer in peers:
            pl.semaphore_signal(sem, inc=1, device_id=peer, device_id_type=MESH)
        pl.semaphore_wait(sem, len(peers))


def each(low, high, body):
    def step(i, carry):
        body(i)
        return carry

    lax.fori_loop(low, high, step, 0)


def gather_kernel(
    grid, enc_ref, w_ref, states_ref, wcat_ref, kv_ref,
    held, weight, raw, wide, total, raw_sem, send_sem, recv_sem, out_sem,
):
    S, Y, Z, C = grid.S, grid.Y, grid.Z, grid.C
    R, F = enc_ref.shape
    depth = weight.shape[0]
    L = weight.shape[1] // 2
    lane_tiles = L // LANES
    x, z, y, c = grid.here()

    def fetch(j):
        return pltpu.make_async_copy(
            w_ref.at[:, :, pl.ds(j * LANES, LANES)], raw.at[j], raw_sem.at[j]
        )

    for j in range(lane_tiles):
        fetch(j).start()
    held[grid.tile(x, z, y, c)] = enc_ref[...]
    total[...] = jnp.zeros_like(total)
    grid.barrier()

    whole = pl.ds(0, R)
    upper, lower = pl.ds(0, R // 2), pl.ds(R // 2, R // 2)
    at_x = Z
    at_y = at_x + (S - 1) * Z
    at_a = at_y + (Y - 1) * Z
    at_b = at_a + (S - 1) * (Y - 1) * Z
    at_s = at_b + (S - 1) * (Y - 1) * Z

    def move(t, rows, target, slot, part=0):
        return pltpu.make_async_remote_copy(
            src_ref=held.at[t, rows],
            dst_ref=held.at[t, rows],
            send_sem=send_sem.at[slot],
            recv_sem=recv_sem.at[part, t],
            device_id=target,
            device_id_type=MESH,
        )

    def arrived(t, rows=whole, part=0):
        move(t, rows, grid.device(wrap(x + 1, S), z, y, c), 0, part).wait_recv()

    def to_sibling(t, dx, dy, dz):
        return [
            move(t, whole, grid.device(x, z, y, wrap(c + d, C)), at_s + (dx * Y + dy) * Z + dz)
            for d in range(1, C)
        ]

    def spread(dz):
        t = grid.tile(x, wrap(z + dz, Z), y, c)
        copies = [
            move(t, whole, grid.device(wrap(x + d, S), z, y, c), at_x + (d - 1) * Z + dz)
            for d in range(1, S)
        ]
        copies += [
            move(t, whole, grid.device(x, z, wrap(y + d, Y), c), at_y + (d - 1) * Z + dz)
            for d in range(1, Y)
        ]
        return copies + to_sibling(t, 0, 0, dz)

    def pass_x(dx, dz):
        t = grid.tile(wrap(x + dx, S), wrap(z + dz, Z), y, c)
        copies = [
            move(t, upper, grid.device(x, z, wrap(y + d, Y), c),
                 at_a + ((dx - 1) * (Y - 1) + d - 1) * Z + dz, 0)
            for d in range(1, Y)
        ]
        return copies + to_sibling(t, dx, 0, dz)

    def pass_y(dy, dz):
        t = grid.tile(x, wrap(z + dz, Z), wrap(y + dy, Y), c)
        copies = [
            move(t, lower, grid.device(wrap(x + d, S), z, y, c),
                 at_b + ((d - 1) * (Y - 1) + dy - 1) * Z + dz, 1)
            for d in range(1, S)
        ]
        return copies + to_sibling(t, 0, dy, dz)

    def start(copies):
        for copy in copies:
            copy.start()

    def done(copies):
        for copy in copies:
            copy.wait_send()

    own = grid.tile(x, z, y, c)

    def along_z(dz):
        return [move(own, whole, grid.device(x, wrap(z + dz, Z), y, c), dz)]

    each(1, Z, lambda dz: start(along_z(dz)))
    start(spread(0))

    def unpack(low, high):
        for j in range(lane_tiles):
            flat = raw.at[j].reshape(2 * depth, LANES)

            def block(i):
                row = pl.multiple_of(i * F, F)
                wide[...] = flat[pl.ds(pl.multiple_of(2 * i * F, 2 * F), 2 * F), :].astype(
                    jnp.float32
                )
                for kind in range(2):
                    first = kind * L + j * LANES
                    weight[pl.ds(row, F), first : first + LANES] = wide[
                        pl.ds(kind, F, stride=2), :
                    ].astype(jnp.bfloat16)

            each(low, high, block)

    blocks = depth // F
    for j in range(lane_tiles):
        fetch(j).wait()
    unpack(0, blocks // 2)

    def column(dz):
        arrived(grid.tile(x, wrap(z + dz, Z), y, c))
        start(spread(dz))

    each(1, Z, column)
    unpack(blocks // 2, blocks)
    weight_out = pltpu.make_async_copy(weight, wcat_ref, out_sem.at[0])
    weight_out.start()

    def multiply(tx, tz, ty, tc):
        row = pl.multiple_of(grid.p(tz, ty, tc) * F, F)
        total[tx] += jnp.dot(
            held[grid.tile(tx, tz, ty, tc)],
            weight[pl.ds(row, F), :],
            preferred_element_type=jnp.float32,
        )

    def sides(dz):
        tz = wrap(z + dz, Z)
        for dx in range(1, S):
            arrived(grid.tile(wrap(x + dx, S), tz, y, c))
            start(pass_x(dx, dz))
        for dy in range(1, Y):
            arrived(grid.tile(x, tz, wrap(y + dy, Y), c))
            start(pass_y(dy, dz))
        multiply(x, tz, y, c)

    each(0, Z, sides)

    def diagonal(dz):
        tz = wrap(z + dz, Z)
        for dx in range(1, S):
            for dy in range(1, Y):
                tx, ty = wrap(x + dx, S), wrap(y + dy, Y)
                t = grid.tile(tx, tz, ty, c)
                arrived(t, upper, 0)
                arrived(t, lower, 1)
                start(to_sibling(t, dx, dy, dz))
        for dx in range(1, S):
            multiply(wrap(x + dx, S), tz, y, c)
        for dy in range(1, Y):
            multiply(x, tz, wrap(y + dy, Y), c)

    each(0, Z, diagonal)

    def rest(dz):
        tz = wrap(z + dz, Z)
        for dx in range(1, S):
            for dy in range(1, Y):
                multiply(wrap(x + dx, S), tz, wrap(y + dy, Y), c)

    each(0, Z, rest)

    for dc in range(1, C):
        for dx in range(S):
            for dy in range(Y):

                def other(dz):
                    tx, tz, ty = wrap(x + dx, S), wrap(z + dz, Z), wrap(y + dy, Y)
                    tc = wrap(c + dc, C)
                    arrived(grid.tile(tx, tz, ty, tc))
                    multiply(tx, tz, ty, tc)

                each(0, Z, other)
    states_out = pltpu.make_async_copy(held, states_ref, out_sem.at[1])
    states_out.start()
    for s in range(S):
        kv_ref[s * R : (s + 1) * R, :] = total[s].astype(jnp.bfloat16)

    each(1, Z, lambda dz: done(along_z(dz)))

    def sent(dz):
        done(spread(dz))
        for dx in range(1, S):
            done(pass_x(dx, dz))
        for dy in range(1, Y):
            done(pass_y(dy, dz))
        for dx in range(1, S):
            for dy in range(1, Y):
                t = grid.tile(wrap(x + dx, S), wrap(z + dz, Z), wrap(y + dy, Y), c)
                done(to_sibling(t, dx, dy, dz))

    each(0, Z, sent)
    weight_out.wait()
    states_out.wait()


def attention_kernel(len_ref, kv_ref, q_ref, g_ref, ctx_ref, qgrad_ref, kvgrad_ref):
    R = kv_ref.shape[0]
    T, L = q_ref.shape
    heads = L // HD
    limit = len_ref[pl.program_id(0)]
    q, g = q_ref[...], g_ref[...]
    keys, values = kv_ref[:, :L], kv_ref[:, L:]
    column = lax.broadcasted_iota(jnp.int32, (R, L), 1)
    pick = [
        jnp.where((column >= h * HD) & (column < (h + 1) * HD), 1.0, 0.0).astype(jnp.float32)
        for h in range(heads)
    ]
    key_stack = jnp.concatenate([keys * m.astype(jnp.bfloat16) for m in pick], axis=0)
    value_stack = jnp.concatenate([values * m.astype(jnp.bfloat16) for m in pick], axis=0)
    factor = HD ** (-0.5)
    f32 = jnp.float32
    scores = lax.dot_general(key_stack, q, NT, preferred_element_type=f32)
    prob_grad = lax.dot_general(value_stack, g, NT, preferred_element_type=f32)
    valid = lax.broadcasted_iota(jnp.int32, (R, T), 0) < limit
    probs, grads = [], []
    for h in range(heads):
        rows = slice(h * R, (h + 1) * R)
        score = jnp.where(valid, scores[rows] * factor, -1e30)
        exponent = jnp.exp(score - jnp.max(score, axis=0, keepdims=True))
        prob = exponent * (1.0 / jnp.sum(exponent, axis=0, keepdims=True))
        part = prob_grad[rows]
        mean = jnp.sum(part * prob, axis=0, keepdims=True)
        probs.append(prob.astype(jnp.bfloat16))
        grads.append((prob * (part - mean) * factor).astype(jnp.bfloat16))
    prob = jnp.concatenate(probs, axis=0)
    grad = jnp.concatenate(grads, axis=0)

    def own_columns(full):
        return sum(pick[h] * full[h * R : (h + 1) * R] for h in range(heads))

    value_grad = own_columns(jnp.dot(prob, g, preferred_element_type=f32))
    key_grad = own_columns(jnp.dot(grad, q, preferred_element_type=f32))
    kvgrad_ref[:, :L] = key_grad.astype(jnp.bfloat16)
    kvgrad_ref[:, L:] = value_grad.astype(jnp.bfloat16)
    ctx_ref[...] = lax.dot_general(prob, value_stack, TN, preferred_element_type=f32).astype(
        jnp.bfloat16
    )
    qgrad_ref[...] = lax.dot_general(grad, key_stack, TN, preferred_element_type=f32).astype(
        jnp.bfloat16
    )


def scatter_kernel(
    grid, kvgrad_ref, wcat_ref, out_ref,
    weight, mine, away, near, diag_a, diag_b, from_x, from_y, from_z, to_z,
    weight_sem, near_send, near_recv, a_send, a_recv, b_send, b_recv,
    x_send, x_recv, y_send, y_recv, z_send, z_recv,
):
    S, Y, Z, C = grid.S, grid.Y, grid.Z, grid.C
    R, F = out_ref.shape
    x, z, y, c = grid.here()
    bf16, f32 = jnp.bfloat16, jnp.float32
    weight_in = pltpu.make_async_copy(wcat_ref, weight, weight_sem.at[0])
    weight_in.start()
    grid.barrier()
    weight_in.wait()

    def term(tz, ty, tc):
        row = pl.multiple_of(grid.p(tz, ty, tc) * F, F)
        full = lax.dot_general(
            kvgrad_ref[...], weight[pl.ds(row, F), :], NT, preferred_element_type=f32
        )
        return full.reshape(S, R, F)

    def remote(src, dst, send, recv, target):
        return pltpu.make_async_remote_copy(
            src_ref=src, dst_ref=dst, send_sem=send, recv_sem=recv,
            device_id=target, device_id_type=MESH,
        )

    def near_copy(i):
        return remote(
            away.at[i], near.at[i], near_send.at[i], near_recv.at[i],
            grid.device(x, z, y, wrap(c + 1, C)),
        )

    def half_a(dx, dy, tz):
        i = ((dy - 1) * (S - 1) + dx - 1) * Z + tz
        ty = wrap(y + dy, Y)
        return remote(
            mine.at[tz * Y + ty, wrap(x + dx, S), pl.ds(0, R // 2)], diag_a.at[i],
            a_send.at[i], a_recv.at[i], grid.device(x, z, ty, c),
        )

    def half_b(dx, dy, tz):
        i = ((dy - 1) * (S - 1) + dx - 1) * Z + tz
        tx = wrap(x + dx, S)
        return remote(
            mine.at[tz * Y + wrap(y + dy, Y), tx, pl.ds(R // 2, R // 2)], diag_b.at[i],
            b_send.at[i], b_recv.at[i], grid.device(tx, z, y, c),
        )

    def along_x(dx, tz):
        i = (dx - 1) * Z + tz
        tx = wrap(x + dx, S)
        return remote(
            mine.at[tz * Y + y, tx], from_x.at[i], x_send.at[i], x_recv.at[i],
            grid.device(tx, z, y, c),
        )

    def along_y(dy, tz):
        i = (dy - 1) * Z + tz
        ty = wrap(y + dy, Y)
        return remote(
            mine.at[tz * Y + ty, x], from_y.at[i], y_send.at[i], y_recv.at[i],
            grid.device(x, z, ty, c),
        )

    def along_z(dz):
        tz = wrap(z + dz, Z)
        return remote(
            to_z.at[dz], from_z.at[dz], z_send.at[dz], z_recv.at[dz],
            grid.device(x, tz, y, c),
        )

    if C > 1:
        for dy in [*range(1, Y), 0]:

            def give(dz):
                tz, ty = wrap(z + dz, Z), wrap(y + dy, Y)
                i = tz * Y + ty
                away[i] = term(tz, ty, wrap(c + 1, C)).astype(bf16)
                near_copy(i).start()

            each(1, Z + 1, give)

    def collect(dz, dy):
        tz, ty = wrap(z + dz, Z), wrap(y + dy, Y)
        i = tz * Y + ty
        value = term(tz, ty, c)
        if C > 1:
            near_copy(i).wait_recv()
            value = value + near[i].astype(f32)
        mine[i] = value.astype(bf16)
        if dy:
            for dx in range(1, S):
                half_a(dx, dy, tz).start()
                half_b(dx, dy, tz).start()

    for dy in [*range(1, Y), 0]:
        each(1, Z + 1, lambda dz: collect(dz, dy))

    def sides(dz):
        tz = wrap(z + dz, Z)
        for dx in range(1, S):
            tx = wrap(x + dx, S)
            for dy in range(1, Y):
                copy = half_a(dx, dy, tz)
                copy.wait_recv()
                i = ((dy - 1) * (S - 1) + dx - 1) * Z + tz
                spot = (tz * Y + y, tx, pl.ds(0, R // 2))
                mine[spot] = (mine[spot].astype(f32) + diag_a[i].astype(f32)).astype(bf16)
            along_x(dx, tz).start()
        for dy in range(1, Y):
            ty = wrap(y + dy, Y)
            for dx in range(1, S):
                half_b(dx, dy, tz).wait_recv()
                i = ((dy - 1) * (S - 1) + dx - 1) * Z + tz
                spot = (tz * Y + ty, x, pl.ds(R // 2, R // 2))
                mine[spot] = (mine[spot].astype(f32) + diag_b[i].astype(f32)).astype(bf16)
            along_y(dy, tz).start()

    each(1, Z + 1, sides)

    def joined(dz):
        tz = wrap(z + dz, Z)
        value = mine[tz * Y + y, x].astype(f32)
        for dx in range(1, S):
            along_x(dx, tz).wait_recv()
            value = value + from_x[(dx - 1) * Z + tz].astype(f32)
        for dy in range(1, Y):
            along_y(dy, tz).wait_recv()
            value = value + from_y[(dy - 1) * Z + tz].astype(f32)
        return value

    def pass_on(dz):
        to_z[dz] = joined(dz).astype(bf16)
        along_z(dz).start()

    each(1, Z, pass_on)
    value = joined(0)
    for dz in range(1, Z):
        along_z(dz).wait_recv()
        value = value + from_z[dz].astype(f32)
    out_ref[...] = value.astype(bf16)

    def sent(tz):
        for dy in range(Y):
            if C > 1:
                near_copy(tz * Y + dy).wait_send()
        for dx in range(1, S):
            along_x(dx, tz).wait_send()
            for dy in range(1, Y):
                half_a(dx, dy, tz).wait_send()
                half_b(dx, dy, tz).wait_send()
        for dy in range(1, Y):
            along_y(dy, tz).wait_send()

    each(0, Z, sent)
    each(1, Z, lambda dz: along_z(dz).wait_send())


def weight_grad_kernel(sections, states_ref, kvgrad_ref, out_ref, packed, wide, sem):
    M, lane_tiles = packed.shape[:2]
    R, F = states_ref.shape[1:]
    L = kvgrad_ref.shape[1] // 2

    def put(p, j):
        return pltpu.make_async_copy(
            packed.at[p, j],
            out_ref.at[pl.ds(pl.multiple_of(p * F, F), F), :, pl.ds(j * LANES, LANES)],
            sem.at[p, j],
        )

    def block(p):
        states = jnp.concatenate([states_ref[s * M + p] for s in range(sections)], axis=0)
        full = lax.dot_general(states, kvgrad_ref[...], TN, preferred_element_type=jnp.float32)
        for j in range(lane_tiles):
            for kind in range(2):
                first = kind * L + j * LANES
                wide[j, pl.ds(kind, F, stride=2), :] = full[:, first : first + LANES]
            packed.at[p, j].reshape(2 * F, LANES)[...] = wide[j].astype(jnp.bfloat16)
            put(p, j).start()

    each(0, M, block)

    def finish(p):
        for j in range(lane_tiles):
            put(p, j).wait()

    each(0, M, finish)


def shards(grid, enc_final, enc_len, kv_weight, queries, d_context):
    S, M, C, Y, Z = grid.S, grid.M, grid.C, grid.Y, grid.Z
    R, F = enc_final.shape[1:]
    D, _, L = kv_weight.shape[1:]
    T = queries.shape[2]
    lane_tiles = L // LANES
    bf16, f32 = jnp.bfloat16, jnp.float32
    dma = pltpu.SemaphoreType.DMA
    vmem = pl.BlockSpec(memory_space=pltpu.VMEM)
    anywhere = pl.BlockSpec(memory_space=pl.ANY)
    shape = jax.ShapeDtypeStruct
    sends = Z + (S - 1) * Z + (Y - 1) * Z + 2 * (S - 1) * (Y - 1) * Z + S * Y * Z
    states, wcat, key_value = pl.pallas_call(
        functools.partial(gather_kernel, grid),
        out_shape=(
            shape((S * M, R, F), bf16), shape((D, 2 * L), bf16), shape((S * R, 2 * L), bf16),
        ),
        in_specs=[vmem, anywhere],
        out_specs=(anywhere, anywhere, vmem),
        scratch_shapes=[
            pltpu.VMEM((S * M, R, F), bf16),
            pltpu.VMEM((D, 2 * L), bf16),
            pltpu.VMEM((lane_tiles, D, 2, LANES), bf16),
            pltpu.VMEM((2 * F, LANES), f32),
            pltpu.VMEM((S, R, 2 * L), f32),
            dma((lane_tiles,)),
            dma((sends,)),
            dma((2, S * M)),
            dma((2,)),
        ],
        compiler_params=pltpu.CompilerParams(
            collective_id=0, has_side_effects=True, vmem_limit_bytes=VMEM_BYTES
        ),
        name="gather_states",
    )(enc_final[0], kv_weight[0])

    rows = pl.BlockSpec((R, 2 * L), lambda m: (m, 0))
    long = pl.BlockSpec((None, T, L), lambda m: (m, 0, 0))
    context, query_grad, kv_grad = pl.pallas_call(
        attention_kernel,
        grid=(S,),
        out_shape=(
            shape((S, T, L), bf16), shape((S, T, L), bf16), shape((S * R, 2 * L), bf16),
        ),
        in_specs=[pl.BlockSpec(memory_space=pltpu.SMEM), rows, long, long],
        out_specs=(long, long, rows),
        compiler_params=pltpu.CompilerParams(vmem_limit_bytes=VMEM_BYTES),
        name="attention",
    )(enc_len, key_value, queries[0], d_context[0])

    pair = max((S - 1) * (Y - 1) * Z, 1)
    enc_grad = pl.pallas_call(
        functools.partial(scatter_kernel, grid),
        out_shape=shape((R, F), bf16),
        in_specs=[vmem, anywhere],
        out_specs=vmem,
        scratch_shapes=[
            pltpu.VMEM((D, 2 * L), bf16),
            pltpu.VMEM((Z * Y, S, R, F), bf16),
            pltpu.VMEM((Z * Y, S, R, F), bf16),
            pltpu.VMEM((Z * Y, S, R, F), bf16),
            pltpu.VMEM((pair, R // 2, F), bf16),
            pltpu.VMEM((pair, R // 2, F), bf16),
            pltpu.VMEM((max(S - 1, 1) * Z, R, F), bf16),
            pltpu.VMEM((max(Y - 1, 1) * Z, R, F), bf16),
            pltpu.VMEM((Z, R, F), bf16),
            pltpu.VMEM((Z, R, F), bf16),
            dma((1,)),
            dma((Z * Y,)), dma((Z * Y,)),
            dma((pair,)), dma((pair,)), dma((pair,)), dma((pair,)),
            dma((max(S - 1, 1) * Z,)), dma((max(S - 1, 1) * Z,)),
            dma((max(Y - 1, 1) * Z,)), dma((max(Y - 1, 1) * Z,)),
            dma((Z,)), dma((Z,)),
        ],
        compiler_params=pltpu.CompilerParams(
            collective_id=1, has_side_effects=True, vmem_limit_bytes=VMEM_BYTES
        ),
        name="scatter_states_grad",
    )(kv_grad, wcat)

    weight_grad = pl.pallas_call(
        functools.partial(weight_grad_kernel, S),
        out_shape=shape((D, 2, L), bf16),
        in_specs=[vmem, vmem],
        out_specs=anywhere,
        scratch_shapes=[
            pltpu.VMEM((M, lane_tiles, F, 2, LANES), bf16),
            pltpu.VMEM((lane_tiles, 2 * F, LANES), f32),
            dma((M, lane_tiles)),
        ],
        compiler_params=pltpu.CompilerParams(vmem_limit_bytes=VMEM_BYTES),
        name="weight_grad",
    )(states, kv_grad)
    return context[None], query_grad[None], weight_grad[None], enc_grad[None]


def solution(mesh):
    grid = Grid(mesh.shape["section"], mesh.shape["mp"])
    split = P("section", None, None, "mp")
    return jax.shard_map(
        functools.partial(shards, grid),
        mesh=mesh,
        in_specs=(P("section", None, "mp"), P(), split, split, split),
        out_specs=(split, split, split, P("section", None, "mp")),
        check_vma=False,
    )
```

time: 157 us -> 63.7 us (0.41)
  waiting for transfers between devices: 78.3 us -> 0 us
  Pallas kernels: 0 us -> 62.1 us
  local copies, waits for them, and re-layouts: 29.3 us -> 0.64 us
  matrix products: 26.7 us -> 0 us
  between operations: 13.9 us -> 0.67 us
  blocking collectives: 7.6 us -> 0 us
    pallas_call x0 -> x4, Pallas kernels: none -> 62.1 us  [the longest x1 28.2 us: shards(): pl.pallas_call(functools.partial(gather_kernel, grid), out_shape=(shape((...]
    reduce_scatter x2 -> x0, waiting for transfers between devices: 51.8 us -> none  [the longest x1 51.8 us: shards(): lax.psum_scatter(full_term.astype(jnp.bfloat16), 'mp', scatter_dimension=...]
    all_gather x1 -> x0, waiting for transfers between devices: 26.5 us -> none  [shards(): states = lax.all_gather(across, 'mp', axis=2, tiled=True)]
    dot_general x8 -> x0, matrix products: 24.5 us -> none  [the longest x1 4.94 us: shards(): jnp.einsum('msk,dk->msd', kv_blocks, weight_flat, preferred_element_type=...]
    unnamed x14 -> x3, local copies, waits for them, and re-layouts: 20.9 us -> 0.64 us
    reshape x2 -> x0, local copies, waits for them, and re-layouts: 7.9 us -> none  [the longest x1 7.63 us: shards(): weight_flat = kv_weight.reshape(model_width, 2 * local_cols)]
    all_gather x1 -> x0, blocking collectives: 7.6 us -> none  [shards(): across = lax.all_gather(enc_final, 'section', axis=0, tiled=True)]
    sub x1 -> x0, matrix products: 2.2 us -> none  [shards(): exponent = jnp.exp(scores - row_peak)]
  transfers between devices with their start and end apart: 3 -> 0, of which waited for: 2 -> 0; matrix products, arithmetic and copies ran while one was open for 25% -> 0% of each run, Pallas kernels for 0% -> 0%
where the time goes in v1:
time: 63.7 us; the launch traced here: 63.4 us
  Pallas kernels  62.1 us (97%)
  between operations  0.67 us (1%)
  local copies, waits for them, and re-layouts  0.64 us (1%)
    pallas_call x1, Pallas kernels, shards(): pl.pallas_call(functools.partial(gather_kernel, grid), out_shape=(shape((...  28.2 us
    pallas_call x1, Pallas kernels, shards(): pl.pallas_call(functools.partial(scatter_kernel, grid), out_shape=shape((...  19.9 us
    pallas_call x1, Pallas kernels, shards(): pl.pallas_call(functools.partial(weight_grad_kernel, S), out_shape=shape(...  9.44 us
    pallas_call x1, Pallas kernels, shards(): pl.pallas_call(attention_kernel, grid=(S,), out_shape=(shape((S, T, L), b...  4.58 us

profile of v1, /device:TPU:0, one launch (start us, length us, event | category | flops | bytes accessed | tf_op | source)
XLA Modules:
  0.0 63.4 jit_solution(13956218952377044587)
XLA Ops:
  0.6 28.2 %gather_states.1 = (bf16[32,128,256]{2,1,0:T(8,128)(2,1)}, bf16[4096,512]{1,0:T(8,128)(2,1)}, bf16[256,512]{1,0:T(8,128)(2,1)}) custom-call(bf16[128,256]{1,0:T(8,128)(2,1)} %bitcast.13, bf16[4096,2,256]{2,1,0:T(2,128)(2,1)} %bitcast.8), custom_call_target="tpu_custom_call" | custom-call | tf_op jit(solution)/shard_map/gather_states/pallas_call | solution.py:518
  28.8 4.6 %attention.1 = (bf16[2,512,256]{2,1,0:T(8,128)(2,1)}, bf16[2,512,256]{2,1,0:T(8,128)(2,1)}, bf16[256,512]{1,0:T(8,128)(2,1)}) custom-call(s32[2]{0:T(128)} %len_ref.1, bf16[256,512]{1,0:T(8,128)(2,1)} %get-tuple-element.10.kv_ref, bf16[2,512,256]{2,1,0:T(8,128)(2,1)} %bitcast.10, bf16[2,512,256]{2,1,0:T(8,128)(2,1)} %bitcast.11), custom_call_target="tpu_custom_call" | custom-call | tf_op jit(solution)/shard_map/attention/pallas_call | solution.py:544
  33.4 19.9 %scatter_states_grad.1 = bf16[128,256]{1,0:T(8,128)(2,1)} custom-call(bf16[256,512]{1,0:T(8,128)(2,1)} %get-tuple-element.14.kvgrad_ref, bf16[4096,512]{1,0:T(8,128)(2,1)} %get-tuple-element.15.wcat_ref), custom_call_target="tpu_custom_call" | custom-call | tf_op jit(solution)/shard_map/scatter_states_grad/pallas_call | solution.py:557
  53.3 0.0 copy-start
  53.4 9.4 %weight_grad.1 = bf16[4096,2,256]{2,1,0:T(2,128)(2,1)} custom-call(bf16[32,128,256]{2,1,0:T(8,128)(2,1)} %get-tuple-element.13.states_ref, bf16[256,512]{1,0:T(8,128)(2,1)} %get-tuple-element.14.kvgrad_ref), custom_call_target="tpu_custom_call" | custom-call | tf_op jit(solution)/shard_map/weight_grad/pallas_call | solution.py:586
  62.8 0.0 copy-done
  62.8 0.6 copy.10
Async XLA Ops:
  53.3 9.5 %copy-start = (bf16[128,256]{1,0:T(8,128)(2,1)S(1)}, bf16[128,256]{1,0:T(8,128)(2,1)}, u32[]{:S(2)}) copy-start(bf16[128,256]{1,0:T(8,128)(2,1)} %scatter_states_grad.1) | copy-start | bytes 196612

commit v2 on v1

--- a/solution.py
+++ b/solution.py
@@ -11,6 +11,7 @@
 LANES = 128
 MESH = pl.DeviceIdType.MESH
 VMEM_BYTES = 56 * 2**20
+UNROLL = 4
 NT = (((1,), (1,)), ((), ()))
 TN = (((0,), (0,)), ((), ()))
 
@@ -36,7 +37,7 @@
         return (z * self.Y + y) * self.C + c
 
     def tile(self, x, z, y, c):
-        return x * self.M + self.p(z, y, c)
+        return x, self.p(z, y, c)
 
     def device(self, x, z, y, c):
         return (x, self.p(z, y, c))
@@ -61,9 +62,16 @@
     lax.fori_loop(low, high, step, 0)
 
 
+def select(back):
+    across = lax.broadcasted_iota(jnp.int32, (2 * LANES, 2 * LANES), 1 - back)
+    along = lax.broadcasted_iota(jnp.int32, (2 * LANES, 2 * LANES), back)
+    source = jnp.where(along < LANES, 2 * along, 2 * (along - LANES) + 1)
+    return jnp.where(across == source, 1.0, 0.0).astype(jnp.float32).astype(jnp.bfloat16)
+
+
 def gather_kernel(
     grid, enc_ref, w_ref, states_ref, wcat_ref, kv_ref,
-    held, weight, raw, wide, total, raw_sem, send_sem, recv_sem, out_sem,
+    held, weight, raw, pick, total, raw_sem, send_sem, recv_sem, out_sem,
 ):
     S, Y, Z, C = grid.S, grid.Y, grid.Z, grid.C
     R, F = enc_ref.shape
@@ -93,10 +101,10 @@
 
     def move(t, rows, target, slot, part=0):
         return pltpu.make_async_remote_copy(
-            src_ref=held.at[t, rows],
-            dst_ref=held.at[t, rows],
+            src_ref=held.at[(*t, rows)],
+            dst_ref=held.at[(*t, rows)],
             send_sem=send_sem.at[slot],
-            recv_sem=recv_sem.at[part, t],
+            recv_sem=recv_sem.at[(part, *t)],
             device_id=target,
             device_id_type=MESH,
         )
@@ -157,23 +165,29 @@
     start(spread(0))
 
     def unpack(low, high):
-        for j in range(lane_tiles):
-            flat = raw.at[j].reshape(2 * depth, LANES)
-
-            def block(i):
-                row = pl.multiple_of(i * F, F)
-                wide[...] = flat[pl.ds(pl.multiple_of(2 * i * F, 2 * F), 2 * F), :].astype(
-                    jnp.float32
+        def block(i):
+            for u in range(UNROLL):
+                group = i * UNROLL + u
+                both = jnp.concatenate(
+                    [
+                        raw.at[j].reshape(2 * depth, LANES)[
+                            pl.ds(pl.multiple_of(group * 2 * LANES, 2 * LANES), 2 * LANES), :
+                        ]
+                        for j in range(lane_tiles)
+                    ],
+                    axis=1,
                 )
-                for kind in range(2):
-                    first = kind * L + j * LANES
-                    weight[pl.ds(row, F), first : first + LANES] = wide[
-                        pl.ds(kind, F, stride=2), :
-                    ].astype(jnp.bfloat16)
-
-            each(low, high, block)
-
-    blocks = depth // F
+                apart = jnp.dot(pick[...], both, preferred_element_type=jnp.float32).astype(
+                    jnp.bfloat16
+                )
+                row = pl.ds(pl.multiple_of(group * LANES, LANES), LANES)
+                weight[row, :L] = apart[:LANES]
+                weight[row, L:] = apart[LANES:]
+
+        each(low, high, block)
+
+    blocks = depth // (LANES * UNROLL)
+    pick[...] = select(0)
     for j in range(lane_tiles):
         fetch(j).wait()
     unpack(0, blocks // 2)
@@ -187,11 +201,11 @@
     weight_out = pltpu.make_async_copy(weight, wcat_ref, out_sem.at[0])
     weight_out.start()
 
-    def multiply(tx, tz, ty, tc):
-        row = pl.multiple_of(grid.p(tz, ty, tc) * F, F)
-        total[tx] += jnp.dot(
-            held[grid.tile(tx, tz, ty, tc)],
-            weight[pl.ds(row, F), :],
+    def multiply(tz, ty, tc):
+        p = grid.p(tz, ty, tc)
+        total[...] += jnp.dot(
+            held[:, p].reshape(S * R, F),
+            weight[pl.ds(pl.multiple_of(p * F, F), F), :],
             preferred_element_type=jnp.float32,
         )
 
@@ -203,49 +217,36 @@
         for dy in range(1, Y):
             arrived(grid.tile(x, tz, wrap(y + dy, Y), c))
             start(pass_y(dy, dz))
-        multiply(x, tz, y, c)
+        multiply(tz, y, c)
 
     each(0, Z, sides)
 
     def diagonal(dz):
         tz = wrap(z + dz, Z)
-        for dx in range(1, S):
-            for dy in range(1, Y):
-                tx, ty = wrap(x + dx, S), wrap(y + dy, Y)
-                t = grid.tile(tx, tz, ty, c)
+        for dy in range(1, Y):
+            ty = wrap(y + dy, Y)
+            for dx in range(1, S):
+                t = grid.tile(wrap(x + dx, S), tz, ty, c)
                 arrived(t, upper, 0)
                 arrived(t, lower, 1)
                 start(to_sibling(t, dx, dy, dz))
-        for dx in range(1, S):
-            multiply(wrap(x + dx, S), tz, y, c)
-        for dy in range(1, Y):
-            multiply(x, tz, wrap(y + dy, Y), c)
+            multiply(tz, ty, c)
 
     each(0, Z, diagonal)
 
-    def rest(dz):
-        tz = wrap(z + dz, Z)
-        for dx in range(1, S):
-            for dy in range(1, Y):
-                multiply(wrap(x + dx, S), tz, wrap(y + dy, Y), c)
-
-    each(0, Z, rest)
-
     for dc in range(1, C):
-        for dx in range(S):
-            for dy in range(Y):
-
-                def other(dz):
-                    tx, tz, ty = wrap(x + dx, S), wrap(z + dz, Z), wrap(y + dy, Y)
-                    tc = wrap(c + dc, C)
-                    arrived(grid.tile(tx, tz, ty, tc))
-                    multiply(tx, tz, ty, tc)
-
-                each(0, Z, other)
+        for dy in range(Y):
+
+            def other(dz):
+                tz, ty, tc = wrap(z + dz, Z), wrap(y + dy, Y), wrap(c + dc, C)
+                for dx in range(S):
+                    arrived(grid.tile(wrap(x + dx, S), tz, ty, tc))
+                multiply(tz, ty, tc)
+
+            each(0, Z, other)
     states_out = pltpu.make_async_copy(held, states_ref, out_sem.at[1])
     states_out.start()
-    for s in range(S):
-        kv_ref[s * R : (s + 1) * R, :] = total[s].astype(jnp.bfloat16)
+    kv_ref[...] = total[...].astype(jnp.bfloat16)
 
     each(1, Z, lambda dz: done(along_z(dz)))
 
@@ -313,10 +314,10 @@
 
 
 def scatter_kernel(
-    grid, kvgrad_ref, wcat_ref, out_ref,
-    weight, mine, away, near, diag_a, diag_b, from_x, from_y, from_z, to_z,
+    grid, kvgrad_ref, wcat_ref, states_ref, out_ref, wgrad_ref,
+    weight, states, packed, pick, mine, away, near, diag_a, diag_b, from_x, from_y, from_z, to_z,
     weight_sem, near_send, near_recv, a_send, a_recv, b_send, b_recv,
-    x_send, x_recv, y_send, y_recv, z_send, z_recv,
+    x_send, x_recv, y_send, y_recv, z_send, z_recv, packed_sem,
 ):
     S, Y, Z, C = grid.S, grid.Y, grid.Z, grid.C
     R, F = out_ref.shape
@@ -324,6 +325,9 @@
     bf16, f32 = jnp.bfloat16, jnp.float32
     weight_in = pltpu.make_async_copy(wcat_ref, weight, weight_sem.at[0])
     weight_in.start()
+    states_in = pltpu.make_async_copy(states_ref, states, weight_sem.at[1])
+    states_in.start()
+    pick[...] = select(1)
     grid.barrier()
     weight_in.wait()
 
@@ -333,6 +337,31 @@
             kvgrad_ref[...], weight[pl.ds(row, F), :], NT, preferred_element_type=f32
         )
         return full.reshape(S, R, F)
+
+    M, lane_tiles = packed.shape[:2]
+    L = lane_tiles * LANES
+
+    def put(p, j):
+        return pltpu.make_async_copy(
+            packed.at[p, j],
+            wgrad_ref.at[pl.ds(pl.multiple_of(p * F, F), F), :, pl.ds(j * LANES, LANES)],
+            packed_sem.at[p, j],
+        )
+
+    def weight_block(p):
+        full = lax.dot_general(
+            states[:, p].reshape(S * R, F), kvgrad_ref[...], TN, preferred_element_type=f32
+        ).astype(bf16)
+        for g in range(F // LANES):
+            rows = full[g * LANES : (g + 1) * LANES]
+            both = jnp.concatenate([rows[:, :L], rows[:, L:]], axis=0)
+            mixed = jnp.dot(pick[...], both, preferred_element_type=f32).astype(bf16)
+            for j in range(lane_tiles):
+                packed.at[p, j].reshape(2 * F, LANES)[
+                    g * 2 * LANES : (g + 1) * 2 * LANES, :
+                ] = mixed[:, j * LANES : (j + 1) * LANES]
+        for j in range(lane_tiles):
+            put(p, j).start()
 
     def remote(src, dst, send, recv, target):
         return pltpu.make_async_remote_copy(
@@ -411,6 +440,10 @@
 
     for dy in [*range(1, Y), 0]:
         each(1, Z + 1, lambda dz: collect(dz, dy))
+
+    states_in.wait()
+    first, second = 3 * M // 16, 10 * M // 16
+    each(0, first, weight_block)
 
     def sides(dz):
         tz = wrap(z + dz, Z)
@@ -433,6 +466,7 @@
             along_y(dy, tz).start()
 
     each(1, Z + 1, sides)
+    each(first, second, weight_block)
 
     def joined(dz):
         tz = wrap(z + dz, Z)
@@ -450,6 +484,7 @@
         along_z(dz).start()
 
     each(1, Z, pass_on)
+    each(second, M, weight_block)
     value = joined(0)
     for dz in range(1, Z):
         along_z(dz).wait_recv()
@@ -471,36 +506,26 @@
     each(0, Z, sent)
     each(1, Z, lambda dz: along_z(dz).wait_send())
 
-
-def weight_grad_kernel(sections, states_ref, kvgrad_ref, out_ref, packed, wide, sem):
-    M, lane_tiles = packed.shape[:2]
-    R, F = states_ref.shape[1:]
-    L = kvgrad_ref.shape[1] // 2
-
-    def put(p, j):
-        return pltpu.make_async_copy(
-            packed.at[p, j],
-            out_ref.at[pl.ds(pl.multiple_of(p * F, F), F), :, pl.ds(j * LANES, LANES)],
-            sem.at[p, j],
-        )
-
-    def block(p):
-        states = jnp.concatenate([states_ref[s * M + p] for s in range(sections)], axis=0)
-        full = lax.dot_general(states, kvgrad_ref[...], TN, preferred_element_type=jnp.float32)
-        for j in range(lane_tiles):
-            for kind in range(2):
-                first = kind * L + j * LANES
-                wide[j, pl.ds(kind, F, stride=2), :] = full[:, first : first + LANES]
-            packed.at[p, j].reshape(2 * F, LANES)[...] = wide[j].astype(jnp.bfloat16)
-            put(p, j).start()
-
-    each(0, M, block)
-
-    def finish(p):
+    def written(p):
         for j in range(lane_tiles):
             put(p, j).wait()
 
-    each(0, M, finish)
+    each(0, M, written)
+
+
+def settle_kernel(from_ref, to_ref, sem):
+    count = sem.shape[0]
+    rows = from_ref.shape[0] // count
+    copies = [
+        pltpu.make_async_copy(
+            from_ref.at[pl.ds(i * rows, rows)], to_ref.at[pl.ds(i * rows, rows)], sem.at[i]
+        )
+        for i in range(count)
+    ]
+    for copy in copies:
+        copy.start()
+    for copy in copies:
+        copy.wait()
 
 
 def shards(grid, enc_final, enc_len, kv_weight, queries, d_context):
@@ -518,19 +543,19 @@
     states, wcat, key_value = pl.pallas_call(
         functools.partial(gather_kernel, grid),
         out_shape=(
-            shape((S * M, R, F), bf16), shape((D, 2 * L), bf16), shape((S * R, 2 * L), bf16),
+            shape((S, M, R, F), bf16), shape((D, 2 * L), bf16), shape((S * R, 2 * L), bf16),
         ),
         in_specs=[vmem, anywhere],
         out_specs=(anywhere, anywhere, vmem),
         scratch_shapes=[
-            pltpu.VMEM((S * M, R, F), bf16),
+            pltpu.VMEM((S, M, R, F), bf16),
             pltpu.VMEM((D, 2 * L), bf16),
             pltpu.VMEM((lane_tiles, D, 2, LANES), bf16),
-            pltpu.VMEM((2 * F, LANES), f32),
-            pltpu.VMEM((S, R, 2 * L), f32),
+            pltpu.VMEM((2 * LANES, 2 * LANES), bf16),
+            pltpu.VMEM((S * R, 2 * L), f32),
             dma((lane_tiles,)),
             dma((sends,)),
-            dma((2, S * M)),
+            dma((2, S, M)),
             dma((2,)),
         ],
         compiler_params=pltpu.CompilerParams(
@@ -554,13 +579,16 @@
     )(enc_len, key_value, queries[0], d_context[0])
 
     pair = max((S - 1) * (Y - 1) * Z, 1)
-    enc_grad = pl.pallas_call(
+    enc_grad, weight_grad = pl.pallas_call(
         functools.partial(scatter_kernel, grid),
-        out_shape=shape((R, F), bf16),
-        in_specs=[vmem, anywhere],
-        out_specs=vmem,
+        out_shape=(shape((R, F), bf16), shape((D, 2, L), bf16)),
+        in_specs=[vmem, anywhere, anywhere],
+        out_specs=(vmem, anywhere),
         scratch_shapes=[
             pltpu.VMEM((D, 2 * L), bf16),
+            pltpu.VMEM((S, M, R, F), bf16),
+            pltpu.VMEM((M, lane_tiles, F, 2, LANES), bf16),
+            pltpu.VMEM((2 * LANES, 2 * LANES), bf16),
             pltpu.VMEM((Z * Y, S, R, F), bf16),
             pltpu.VMEM((Z * Y, S, R, F), bf16),
             pltpu.VMEM((Z * Y, S, R, F), bf16),
@@ -570,32 +598,27 @@
             pltpu.VMEM((max(Y - 1, 1) * Z, R, F), bf16),
             pltpu.VMEM((Z, R, F), bf16),
             pltpu.VMEM((Z, R, F), bf16),
-            dma((1,)),
+            dma((2,)),
             dma((Z * Y,)), dma((Z * Y,)),
             dma((pair,)), dma((pair,)), dma((pair,)), dma((pair,)),
             dma((max(S - 1, 1) * Z,)), dma((max(S - 1, 1) * Z,)),
             dma((max(Y - 1, 1) * Z,)), dma((max(Y - 1, 1) * Z,)),
-            dma((Z,)), dma((Z,)),
+            dma((Z,)), dma((Z,)), dma((M, lane_tiles)),
         ],
         compiler_params=pltpu.CompilerParams(
             collective_id=1, has_side_effects=True, vmem_limit_bytes=VMEM_BYTES
         ),
         name="scatter_states_grad",
-    )(kv_grad, wcat)
+    )(kv_grad, wcat, states)
 
     weight_grad = pl.pallas_call(
-        functools.partial(weight_grad_kernel, S),
+        settle_kernel,
         out_shape=shape((D, 2, L), bf16),
-        in_specs=[vmem, vmem],
+        in_specs=[anywhere],
         out_specs=anywhere,
-        scratch_shapes=[
-            pltpu.VMEM((M, lane_tiles, F, 2, LANES), bf16),
-            pltpu.VMEM((lane_tiles, 2 * F, LANES), f32),
-            dma((M, lane_tiles)),
-        ],
-        compiler_params=pltpu.CompilerParams(vmem_limit_bytes=VMEM_BYTES),
-        name="weight_grad",
-    )(states, kv_grad)
+        scratch_shapes=[dma((8,))],
+        name="settle_weight_grad",
+    )(weight_grad)
     return context[None], query_grad[None], weight_grad[None], enc_grad[None]
 
 

time: 63.7 us -> 182 us (2.86)
  Pallas kernels: 62.1 us -> 180 us
    pallas_call x2, Pallas kernels: 29.4 us -> 150 us  [the longest x1 128 us: shards(): pl.pallas_call(settle_kernel, out_shape=shape((D, 2, L), bf16), in_specs=...]
    pallas_call x1, Pallas kernels: 28.2 us -> 26.2 us  [shards(): pl.pallas_call(functools.partial(gather_kernel, grid), out_shape=(shape((...]
where the time goes in v2:
time: 182 us
  Pallas kernels  180 us (99%)
    pallas_call x1, Pallas kernels, shards(): pl.pallas_call(settle_kernel, out_shape=shape((D, 2, L), bf16), in_specs=...  128 us
    pallas_call x1, Pallas kernels, shards(): pl.pallas_call(functools.partial(gather_kernel, grid), out_shape=(shape((...  26.2 us
    pallas_call x1, Pallas kernels, shards(): pl.pallas_call(functools.partial(scatter_kernel, grid), out_shape=(shape(...  21.4 us
    pallas_call x1, Pallas kernels, shards(): pl.pallas_call(attention_kernel, grid=(S,), out_shape=(shape((S, T, L), b...  4.6 us

profile of v2, /device:TPU:0, one launch (start us, length us, event | category | flops | bytes accessed | tf_op | source)
XLA Modules:
  0.0 181.7 jit_solution(11306146260128241856)
XLA Ops:
  0.6 26.2 %gather_states.1 = (bf16[2,16,128,256]{3,2,1,0:T(8,128)(2,1)}, bf16[4096,512]{1,0:T(8,128)(2,1)}, bf16[256,512]{1,0:T(8,128)(2,1)}) custom-call(bf16[128,256]{1,0:T(8,128)(2,1)} %bitcast.12, bf16[4096,2,256]{2,1,0:T(2,128)(2,1)} %bitcast.8), custom_call_target="tpu_custom_call" | custom-call | tf_op jit(solution)/shard_map/gather_states/pallas_call | solution.py:543
  26.8 4.6 %attention.1 = (bf16[2,512,256]{2,1,0:T(8,128)(2,1)}, bf16[2,512,256]{2,1,0:T(8,128)(2,1)}, bf16[256,512]{1,0:T(8,128)(2,1)}) custom-call(s32[2]{0:T(128)} %len_ref.1, bf16[256,512]{1,0:T(8,128)(2,1)} %get-tuple-element.12.kv_ref, bf16[2,512,256]{2,1,0:T(8,128)(2,1)} %bitcast.10, bf16[2,512,256]{2,1,0:T(8,128)(2,1)} %bitcast.11), custom_call_target="tpu_custom_call" | custom-call | tf_op jit(solution)/shard_map/attention/pallas_call | solution.py:569
  31.4 21.4 %scatter_states_grad.1 = (bf16[128,256]{1,0:T(8,128)(2,1)}, bf16[4096,2,256]{2,1,0:T(2,128)(2,1)}) custom-call(bf16[256,512]{1,0:T(8,128)(2,1)} %get-tuple-element.15.kvgrad_ref, bf16[4096,512]{1,0:T(8,128)(2,1)} %get-tuple-element.16.wcat_ref, bf16[2,16,128,256]{3,2,1,0:T(8,128)(2,1)} %get-tuple-element.17.states_ref), custom_call_target="tpu_custom_call" | custom-call | tf_op jit(solution)/shard_map/scatter_states_grad/pallas_call | solution.py:582
  52.8 0.0 copy-start
  52.8 128.2 %settle_weight_grad.1 = bf16[4096,2,256]{2,1,0:T(2,128)(2,1)} custom-call(bf16[4096,2,256]{2,1,0:T(2,128)(2,1)} %get-tuple-element.18.from_ref), custom_call_target="tpu_custom_call" | custom-call | tf_op jit(solution)/shard_map/settle_weight_grad/pallas_call | solution.py:614
  181.1 0.0 copy-done
  181.1 0.6 copy.10
Async XLA Ops:
  52.8 128.3 %copy-start = (bf16[128,256]{1,0:T(8,128)(2,1)S(1)}, bf16[128,256]{1,0:T(8,128)(2,1)}, u32[]{:S(2)}) copy-start(bf16[128,256]{1,0:T(8,128)(2,1)} %get-tuple-element.19) | copy-start | bytes 196612

commit v3 on v2

--- a/solution.py
+++ b/solution.py
@@ -62,11 +62,19 @@
     lax.fori_loop(low, high, step, 0)
 
 
-def select(back):
-    across = lax.broadcasted_iota(jnp.int32, (2 * LANES, 2 * LANES), 1 - back)
-    along = lax.broadcasted_iota(jnp.int32, (2 * LANES, 2 * LANES), back)
-    source = jnp.where(along < LANES, 2 * along, 2 * (along - LANES) + 1)
-    return jnp.where(across == source, 1.0, 0.0).astype(jnp.float32).astype(jnp.bfloat16)
+def select(lane_tiles, back):
+    size = 2 * LANES
+    count = size // (2 * lane_tiles)
+    across = lax.broadcasted_iota(jnp.int32, (size, size), 1 - back)
+    along = lax.broadcasted_iota(jnp.int32, (size, size), back)
+    hit = jnp.zeros((size, size), jnp.float32)
+    for kind in range(2):
+        for j in range(lane_tiles):
+            low = (kind * lane_tiles + j) * count
+            source = (along - low) * (2 * lane_tiles) + 2 * j + kind
+            inside = (along >= low) & (along < low + count)
+            hit = jnp.where(inside & (across == source), 1.0, hit)
+    return hit.astype(jnp.bfloat16)
 
 
 def gather_kernel(
@@ -80,13 +88,15 @@
     lane_tiles = L // LANES
     x, z, y, c = grid.here()
 
-    def fetch(j):
-        return pltpu.make_async_copy(
-            w_ref.at[:, :, pl.ds(j * LANES, LANES)], raw.at[j], raw_sem.at[j]
-        )
-
-    for j in range(lane_tiles):
-        fetch(j).start()
+    parts = raw_sem.shape[0]
+    part_rows = raw.shape[0] // parts
+
+    def fetch(i):
+        rows = pl.ds(i * part_rows, part_rows)
+        return pltpu.make_async_copy(w_ref.at[rows], raw.at[rows], raw_sem.at[i])
+
+    for i in range(parts):
+        fetch(i).start()
     held[grid.tile(x, z, y, c)] = enc_ref[...]
     total[...] = jnp.zeros_like(total)
     grid.barrier()
@@ -164,32 +174,37 @@
     each(1, Z, lambda dz: start(along_z(dz)))
     start(spread(0))
 
+    size = 2 * LANES
+    count = size // (2 * lane_tiles)
+    flat = raw.reshape(depth * lane_tiles * 2, LANES)
+
     def unpack(low, high):
         def block(i):
             for u in range(UNROLL):
-                group = i * UNROLL + u
+                first = (i * UNROLL + u) * 2
                 both = jnp.concatenate(
                     [
-                        raw.at[j].reshape(2 * depth, LANES)[
-                            pl.ds(pl.multiple_of(group * 2 * LANES, 2 * LANES), 2 * LANES), :
-                        ]
-                        for j in range(lane_tiles)
+                        flat[pl.ds(pl.multiple_of((first + k) * size, size), size), :]
+                        for k in range(2)
                     ],
                     axis=1,
                 )
                 apart = jnp.dot(pick[...], both, preferred_element_type=jnp.float32).astype(
                     jnp.bfloat16
                 )
-                row = pl.ds(pl.multiple_of(group * LANES, LANES), LANES)
-                weight[row, :L] = apart[:LANES]
-                weight[row, L:] = apart[LANES:]
+                for k in range(2):
+                    row = pl.ds(pl.multiple_of((first + k) * count, count), count)
+                    for col in range(2 * lane_tiles):
+                        weight[row, col * LANES : (col + 1) * LANES] = apart[
+                            col * count : (col + 1) * count, k * LANES : (k + 1) * LANES
+                        ]
 
         each(low, high, block)
 
-    blocks = depth // (LANES * UNROLL)
-    pick[...] = select(0)
-    for j in range(lane_tiles):
-        fetch(j).wait()
+    blocks = depth // (count * 2 * UNROLL)
+    pick[...] = select(lane_tiles, 0)
+    for i in range(parts // 2):
+        fetch(i).wait()
     unpack(0, blocks // 2)
 
     def column(dz):
@@ -197,6 +212,8 @@
         start(spread(dz))
 
     each(1, Z, column)
+    for i in range(parts // 2, parts):
+        fetch(i).wait()
     unpack(blocks // 2, blocks)
     weight_out = pltpu.make_async_copy(weight, wcat_ref, out_sem.at[0])
     weight_out.start()
@@ -327,7 +344,7 @@
     weight_in.start()
     states_in = pltpu.make_async_copy(states_ref, states, weight_sem.at[1])
     states_in.start()
-    pick[...] = select(1)
+    pick[...] = select(packed.shape[1] // F, 1)
     grid.barrier()
     weight_in.wait()
 
@@ -338,30 +355,44 @@
         )
         return full.reshape(S, R, F)
 
-    M, lane_tiles = packed.shape[:2]
-    L = lane_tiles * LANES
-
-    def put(p, j):
+    M, tall = packed.shape[:2]
+    lane_tiles = tall // F
+    size = 2 * LANES
+    count = size // (2 * lane_tiles)
+    beside = 2 if F % (2 * count) == 0 else 1
+
+    def put(p):
         return pltpu.make_async_copy(
-            packed.at[p, j],
-            wgrad_ref.at[pl.ds(pl.multiple_of(p * F, F), F), :, pl.ds(j * LANES, LANES)],
-            packed_sem.at[p, j],
+            packed.at[p],
+            wgrad_ref.at[pl.ds(pl.multiple_of(p * tall, tall), tall)],
+            packed_sem.at[p],
         )
 
     def weight_block(p):
         full = lax.dot_general(
             states[:, p].reshape(S * R, F), kvgrad_ref[...], TN, preferred_element_type=f32
         ).astype(bf16)
-        for g in range(F // LANES):
-            rows = full[g * LANES : (g + 1) * LANES]
-            both = jnp.concatenate([rows[:, :L], rows[:, L:]], axis=0)
+        flat = packed.at[p].reshape(2 * tall, LANES)
+        for g in range(0, F // count, beside):
+            both = jnp.concatenate(
+                [
+                    jnp.concatenate(
+                        [
+                            full[k * count : (k + 1) * count, col * LANES : (col + 1) * LANES]
+                            for col in range(2 * lane_tiles)
+                        ],
+                        axis=0,
+                    )
+                    for k in range(g, g + beside)
+                ],
+                axis=1,
+            )
             mixed = jnp.dot(pick[...], both, preferred_element_type=f32).astype(bf16)
-            for j in range(lane_tiles):
-                packed.at[p, j].reshape(2 * F, LANES)[
-                    g * 2 * LANES : (g + 1) * 2 * LANES, :
-                ] = mixed[:, j * LANES : (j + 1) * LANES]
-        for j in range(lane_tiles):
-            put(p, j).start()
+            for k in range(beside):
+                flat[(g + k) * size : (g + k + 1) * size, :] = mixed[
+                    :, k * LANES : (k + 1) * LANES
+                ]
+        put(p).start()
 
     def remote(src, dst, send, recv, target):
         return pltpu.make_async_remote_copy(
@@ -507,25 +538,29 @@
     each(1, Z, lambda dz: along_z(dz).wait_send())
 
     def written(p):
-        for j in range(lane_tiles):
-            put(p, j).wait()
+        put(p).wait()
 
     each(0, M, written)
 
 
-def settle_kernel(from_ref, to_ref, sem):
-    count = sem.shape[0]
-    rows = from_ref.shape[0] // count
-    copies = [
-        pltpu.make_async_copy(
-            from_ref.at[pl.ds(i * rows, rows)], to_ref.at[pl.ds(i * rows, rows)], sem.at[i]
-        )
-        for i in range(count)
-    ]
-    for copy in copies:
-        copy.start()
-    for copy in copies:
-        copy.wait()
+def settle_kernel(from_ref, to_ref, held, in_sem, out_sem):
+    parts = in_sem.shape[0]
+    part_rows = held.shape[0] // parts
+
+    def copies(i):
+        rows = pl.ds(i * part_rows, part_rows)
+        return (
+            pltpu.make_async_copy(from_ref.at[rows], held.at[rows], in_sem.at[i]),
+            pltpu.make_async_copy(held.at[rows], to_ref.at[rows], out_sem.at[i]),
+        )
+
+    for i in range(parts):
+        copies(i)[0].start()
+    for i in range(parts):
+        copies(i)[0].wait()
+        copies(i)[1].start()
+    for i in range(parts):
+        copies(i)[1].wait()
 
 
 def shards(grid, enc_final, enc_len, kv_weight, queries, d_context):
@@ -539,6 +574,9 @@
     vmem = pl.BlockSpec(memory_space=pltpu.VMEM)
     anywhere = pl.BlockSpec(memory_space=pl.ANY)
     shape = jax.ShapeDtypeStruct
+    by_lane_tile = (
+        kv_weight[0].reshape(D, 2, lane_tiles, LANES).transpose(0, 2, 1, 3)
+    ).reshape(D * lane_tiles, 2, LANES)
     sends = Z + (S - 1) * Z + (Y - 1) * Z + 2 * (S - 1) * (Y - 1) * Z + S * Y * Z
     states, wcat, key_value = pl.pallas_call(
         functools.partial(gather_kernel, grid),
@@ -550,10 +588,10 @@
         scratch_shapes=[
             pltpu.VMEM((S, M, R, F), bf16),
             pltpu.VMEM((D, 2 * L), bf16),
-            pltpu.VMEM((lane_tiles, D, 2, LANES), bf16),
+            pltpu.VMEM((D * lane_tiles, 2, LANES), bf16),
             pltpu.VMEM((2 * LANES, 2 * LANES), bf16),
             pltpu.VMEM((S * R, 2 * L), f32),
-            dma((lane_tiles,)),
+            dma((4,)),
             dma((sends,)),
             dma((2, S, M)),
             dma((2,)),
@@ -562,7 +600,7 @@
             collective_id=0, has_side_effects=True, vmem_limit_bytes=VMEM_BYTES
         ),
         name="gather_states",
-    )(enc_final[0], kv_weight[0])
+    )(enc_final[0], by_lane_tile)
 
     rows = pl.BlockSpec((R, 2 * L), lambda m: (m, 0))
     long = pl.BlockSpec((None, T, L), lambda m: (m, 0, 0))
@@ -581,13 +619,13 @@
     pair = max((S - 1) * (Y - 1) * Z, 1)
     enc_grad, weight_grad = pl.pallas_call(
         functools.partial(scatter_kernel, grid),
-        out_shape=(shape((R, F), bf16), shape((D, 2, L), bf16)),
+        out_shape=(shape((R, F), bf16), shape((D * lane_tiles, 2, LANES), bf16)),
         in_specs=[vmem, anywhere, anywhere],
         out_specs=(vmem, anywhere),
         scratch_shapes=[
             pltpu.VMEM((D, 2 * L), bf16),
             pltpu.VMEM((S, M, R, F), bf16),
-            pltpu.VMEM((M, lane_tiles, F, 2, LANES), bf16),
+            pltpu.VMEM((M, F * lane_tiles, 2, LANES), bf16),
             pltpu.VMEM((2 * LANES, 2 * LANES), bf16),
             pltpu.VMEM((Z * Y, S, R, F), bf16),
             pltpu.VMEM((Z * Y, S, R, F), bf16),
@@ -603,7 +641,7 @@
             dma((pair,)), dma((pair,)), dma((pair,)), dma((pair,)),
             dma((max(S - 1, 1) * Z,)), dma((max(S - 1, 1) * Z,)),
             dma((max(Y - 1, 1) * Z,)), dma((max(Y - 1, 1) * Z,)),
-            dma((Z,)), dma((Z,)), dma((M, lane_tiles)),
+            dma((Z,)), dma((Z,)), dma((M,)),
         ],
         compiler_params=pltpu.CompilerParams(
             collective_id=1, has_side_effects=True, vmem_limit_bytes=VMEM_BYTES
@@ -613,12 +651,16 @@
 
     weight_grad = pl.pallas_call(
         settle_kernel,
-        out_shape=shape((D, 2, L), bf16),
+        out_shape=shape((D * lane_tiles, 2, LANES), bf16),
         in_specs=[anywhere],
         out_specs=anywhere,
-        scratch_shapes=[dma((8,))],
+        scratch_shapes=[pltpu.VMEM((D * lane_tiles, 2, LANES), bf16), dma((8,)), dma((8,))],
+        compiler_params=pltpu.CompilerParams(vmem_limit_bytes=VMEM_BYTES),
         name="settle_weight_grad",
     )(weight_grad)
+    weight_grad = (
+        weight_grad.reshape(D, lane_tiles, 2, LANES).transpose(0, 2, 1, 3).reshape(D, 2, L)
+    )
     return context[None], query_grad[None], weight_grad[None], enc_grad[None]
 
 

time: 182 us -> 57.2 us (0.31)
  Pallas kernels: 180 us -> 55.7 us
    pallas_call x1, Pallas kernels: 128 us -> 3.61 us  [shards(): pl.pallas_call(settle_kernel, out_shape=shape((D * lane_tiles, 2, LANES),...]
where the time goes in v3:
time: 57.2 us; the launch traced here: 57 us
  Pallas kernels  55.7 us (97%)
  between operations  0.67 us (1%)
  local copies, waits for them, and re-layouts  0.64 us (1%)
    pallas_call x1, Pallas kernels, shards(): pl.pallas_call(functools.partial(gather_kernel, grid), out_shape=(shape((...  26.2 us
    pallas_call x1, Pallas kernels, shards(): pl.pallas_call(functools.partial(scatter_kernel, grid), out_shape=(shape(...  21.3 us
    pallas_call x1, Pallas kernels, shards(): pl.pallas_call(attention_kernel, grid=(S,), out_shape=(shape((S, T, L), b...  4.59 us
    pallas_call x1, Pallas kernels, shards(): pl.pallas_call(settle_kernel, out_shape=shape((D * lane_tiles, 2, LANES),...  3.61 us

profile of v3, /device:TPU:0, one launch (start us, length us, event | category | flops | bytes accessed | tf_op | source)
XLA Modules:
  0.0 57.0 jit_solution(6222647106097517030)
XLA Ops:
  0.6 26.2 %gather_states.1 = (bf16[2,16,128,256]{3,2,1,0:T(8,128)(2,1)}, bf16[4096,512]{1,0:T(8,128)(2,1)}, bf16[256,512]{1,0:T(8,128)(2,1)}) custom-call(bf16[128,256]{1,0:T(8,128)(2,1)} %bitcast.20, bf16[8192,2,128]{2,1,0:T(2,128)(2,1)} %bitcast.16), custom_call_target="tpu_custom_call" | custom-call | tf_op jit(solution)/shard_map/gather_states/pallas_call | solution.py:581
  26.9 4.6 %attention.1 = (bf16[2,512,256]{2,1,0:T(8,128)(2,1)}, bf16[2,512,256]{2,1,0:T(8,128)(2,1)}, bf16[256,512]{1,0:T(8,128)(2,1)}) custom-call(s32[2]{0:T(128)} %len_ref.1, bf16[256,512]{1,0:T(8,128)(2,1)} %get-tuple-element.12.kv_ref, bf16[2,512,256]{2,1,0:T(8,128)(2,1)} %bitcast.18, bf16[2,512,256]{2,1,0:T(8,128)(2,1)} %bitcast.19), custom_call_target="tpu_custom_call" | custom-call | tf_op jit(solution)/shard_map/attention/pallas_call | solution.py:607
  31.4 21.3 %scatter_states_grad.1 = (bf16[128,256]{1,0:T(8,128)(2,1)}, bf16[8192,2,128]{2,1,0:T(2,128)(2,1)}) custom-call(bf16[256,512]{1,0:T(8,128)(2,1)} %get-tuple-element.15.kvgrad_ref, bf16[4096,512]{1,0:T(8,128)(2,1)} %get-tuple-element.16.wcat_ref, bf16[2,16,128,256]{3,2,1,0:T(8,128)(2,1)} %get-tuple-element.17.states_ref), custom_call_target="tpu_custom_call" | custom-call | tf_op jit(solution)/shard_map/scatter_states_grad/pallas_call | solution.py:620
  52.8 0.0 copy-start
  52.8 3.6 %settle_weight_grad.1 = bf16[8192,2,128]{2,1,0:T(2,128)(2,1)} custom-call(bf16[8192,2,128]{2,1,0:T(2,128)(2,1)} %get-tuple-element.18.from_ref), custom_call_target="tpu_custom_call" | custom-call | tf_op jit(solution)/shard_map/settle_weight_grad/pallas_call | solution.py:652
  56.4 0.0 copy-done
  56.4 0.6 %copy.12 = bf16[1,128,256]{2,1,0:T(8,128)(2,1)} copy(bf16[1,128,256]{2,1,0:T(8,128)(2,1)S(1)} %bitcast.21) | data formatting | bytes 131072
Async XLA Ops:
  52.8 3.6 %copy-start = (bf16[128,256]{1,0:T(8,128)(2,1)S(1)}, bf16[128,256]{1,0:T(8,128)(2,1)}, u32[]{:S(2)}) copy-start(bf16[128,256]{1,0:T(8,128)(2,1)} %get-tuple-element.19) | copy-start | bytes 196612

commit v4 on v3

--- a/solution.py
+++ b/solution.py
@@ -77,9 +77,8 @@
     return hit.astype(jnp.bfloat16)
 
 
-def gather_kernel(
-    grid, enc_ref, w_ref, states_ref, wcat_ref, kv_ref,
-    held, weight, raw, pick, total, raw_sem, send_sem, recv_sem, out_sem,
+def gather(
+    grid, enc_ref, w_ref, kv_ref, held, weight, raw, pick, total, raw_sem, send_sem, recv_sem,
 ):
     S, Y, Z, C = grid.S, grid.Y, grid.Z, grid.C
     R, F = enc_ref.shape
@@ -215,8 +214,6 @@
     for i in range(parts // 2, parts):
         fetch(i).wait()
     unpack(blocks // 2, blocks)
-    weight_out = pltpu.make_async_copy(weight, wcat_ref, out_sem.at[0])
-    weight_out.start()
 
     def multiply(tz, ty, tc):
         p = grid.p(tz, ty, tc)
@@ -261,11 +258,7 @@
                 multiply(tz, ty, tc)
 
             each(0, Z, other)
-    states_out = pltpu.make_async_copy(held, states_ref, out_sem.at[1])
-    states_out.start()
     kv_ref[...] = total[...].astype(jnp.bfloat16)
-
-    each(1, Z, lambda dz: done(along_z(dz)))
 
     def sent(dz):
         done(spread(dz))
@@ -278,75 +271,82 @@
                 t = grid.tile(wrap(x + dx, S), wrap(z + dz, Z), wrap(y + dy, Y), c)
                 done(to_sibling(t, dx, dy, dz))
 
-    each(0, Z, sent)
-    weight_out.wait()
-    states_out.wait()
-
-
-def attention_kernel(len_ref, kv_ref, q_ref, g_ref, ctx_ref, qgrad_ref, kvgrad_ref):
-    R = kv_ref.shape[0]
-    T, L = q_ref.shape
+    def finish():
+        each(1, Z, lambda dz: done(along_z(dz)))
+        each(0, Z, sent)
+
+    return finish
+
+
+def head_columns(R, L):
+    column = lax.broadcasted_iota(jnp.int32, (R, L), 1)
+    return [
+        jnp.where((column >= h * HD) & (column < (h + 1) * HD), 1.0, 0.0).astype(jnp.float32)
+        for h in range(L // HD)
+    ]
+
+
+def stack_heads(block):
+    pick = head_columns(*block.shape)
+    return jnp.concatenate([block * m.astype(block.dtype) for m in pick], axis=0)
+
+
+def attention_grads(m, R, len_ref, kv_ref, q_ref, g_ref, prob_ref, grad_ref, kvgrad_ref):
+    T, L = q_ref.shape[1:]
     heads = L // HD
-    limit = len_ref[pl.program_id(0)]
-    q, g = q_ref[...], g_ref[...]
-    keys, values = kv_ref[:, :L], kv_ref[:, L:]
-    column = lax.broadcasted_iota(jnp.int32, (R, L), 1)
-    pick = [
-        jnp.where((column >= h * HD) & (column < (h + 1) * HD), 1.0, 0.0).astype(jnp.float32)
-        for h in range(heads)
-    ]
-    key_stack = jnp.concatenate([keys * m.astype(jnp.bfloat16) for m in pick], axis=0)
-    value_stack = jnp.concatenate([values * m.astype(jnp.bfloat16) for m in pick], axis=0)
+    rows = pl.ds(pl.multiple_of(m * R, R), R)
+    limit = len_ref[m]
+    q, g = q_ref[m], g_ref[m]
     factor = HD ** (-0.5)
     f32 = jnp.float32
-    scores = lax.dot_general(key_stack, q, NT, preferred_element_type=f32)
-    prob_grad = lax.dot_general(value_stack, g, NT, preferred_element_type=f32)
+    scores = lax.dot_general(stack_heads(kv_ref[rows, :L]), q, NT, preferred_element_type=f32)
+    prob_grad = lax.dot_general(
+        stack_heads(kv_ref[rows, L:]), g, NT, preferred_element_type=f32
+    )
     valid = lax.broadcasted_iota(jnp.int32, (R, T), 0) < limit
-    probs, grads = [], []
     for h in range(heads):
-        rows = slice(h * R, (h + 1) * R)
-        score = jnp.where(valid, scores[rows] * factor, -1e30)
+        own = slice(h * R, (h + 1) * R)
+        score = jnp.where(valid, scores[own] * factor, -1e30)
         exponent = jnp.exp(score - jnp.max(score, axis=0, keepdims=True))
         prob = exponent * (1.0 / jnp.sum(exponent, axis=0, keepdims=True))
-        part = prob_grad[rows]
+        part = prob_grad[own]
         mean = jnp.sum(part * prob, axis=0, keepdims=True)
-        probs.append(prob.astype(jnp.bfloat16))
-        grads.append((prob * (part - mean) * factor).astype(jnp.bfloat16))
-    prob = jnp.concatenate(probs, axis=0)
-    grad = jnp.concatenate(grads, axis=0)
+        prob_ref[m, own] = prob.astype(jnp.bfloat16)
+        grad_ref[m, own] = (prob * (part - mean) * factor).astype(jnp.bfloat16)
+    pick = head_columns(R, L)
 
     def own_columns(full):
         return sum(pick[h] * full[h * R : (h + 1) * R] for h in range(heads))
 
-    value_grad = own_columns(jnp.dot(prob, g, preferred_element_type=f32))
-    key_grad = own_columns(jnp.dot(grad, q, preferred_element_type=f32))
-    kvgrad_ref[:, :L] = key_grad.astype(jnp.bfloat16)
-    kvgrad_ref[:, L:] = value_grad.astype(jnp.bfloat16)
-    ctx_ref[...] = lax.dot_general(prob, value_stack, TN, preferred_element_type=f32).astype(
-        jnp.bfloat16
-    )
-    qgrad_ref[...] = lax.dot_general(grad, key_stack, TN, preferred_element_type=f32).astype(
-        jnp.bfloat16
-    )
-
-
-def scatter_kernel(
-    grid, kvgrad_ref, wcat_ref, states_ref, out_ref, wgrad_ref,
+    value_grad = own_columns(jnp.dot(prob_ref[m], g, preferred_element_type=f32))
+    key_grad = own_columns(jnp.dot(grad_ref[m], q, preferred_element_type=f32))
+    kvgrad_ref[rows, :L] = key_grad.astype(jnp.bfloat16)
+    kvgrad_ref[rows, L:] = value_grad.astype(jnp.bfloat16)
+
+
+def attention_outputs(m, R, kv_ref, prob_ref, grad_ref, ctx_ref, qgrad_ref):
+    L = ctx_ref.shape[2]
+    rows = pl.ds(pl.multiple_of(m * R, R), R)
+    f32 = jnp.float32
+    ctx_ref[m] = lax.dot_general(
+        prob_ref[m], stack_heads(kv_ref[rows, L:]), TN, preferred_element_type=f32
+    ).astype(jnp.bfloat16)
+    qgrad_ref[m] = lax.dot_general(
+        grad_ref[m], stack_heads(kv_ref[rows, :L]), TN, preferred_element_type=f32
+    ).astype(jnp.bfloat16)
+
+
+def scatter(
+    grid, kvgrad_ref, out_ref, wgrad_ref, while_moving,
     weight, states, packed, pick, mine, away, near, diag_a, diag_b, from_x, from_y, from_z, to_z,
-    weight_sem, near_send, near_recv, a_send, a_recv, b_send, b_recv,
+    near_send, near_recv, a_send, a_recv, b_send, b_recv,
     x_send, x_recv, y_send, y_recv, z_send, z_recv, packed_sem,
 ):
     S, Y, Z, C = grid.S, grid.Y, grid.Z, grid.C
     R, F = out_ref.shape
     x, z, y, c = grid.here()
     bf16, f32 = jnp.bfloat16, jnp.float32
-    weight_in = pltpu.make_async_copy(wcat_ref, weight, weight_sem.at[0])
-    weight_in.start()
-    states_in = pltpu.make_async_copy(states_ref, states, weight_sem.at[1])
-    states_in.start()
     pick[...] = select(packed.shape[1] // F, 1)
-    grid.barrier()
-    weight_in.wait()
 
     def term(tz, ty, tc):
         row = pl.multiple_of(grid.p(tz, ty, tc) * F, F)
@@ -472,7 +472,7 @@
     for dy in [*range(1, Y), 0]:
         each(1, Z + 1, lambda dz: collect(dz, dy))
 
-    states_in.wait()
+    while_moving()
     first, second = 3 * M // 16, 10 * M // 16
     each(0, first, weight_block)
 
@@ -543,24 +543,65 @@
     each(0, M, written)
 
 
-def settle_kernel(from_ref, to_ref, held, in_sem, out_sem):
-    parts = in_sem.shape[0]
-    part_rows = held.shape[0] // parts
-
-    def copies(i):
-        rows = pl.ds(i * part_rows, part_rows)
-        return (
-            pltpu.make_async_copy(from_ref.at[rows], held.at[rows], in_sem.at[i]),
-            pltpu.make_async_copy(held.at[rows], to_ref.at[rows], out_sem.at[i]),
-        )
-
-    for i in range(parts):
-        copies(i)[0].start()
-    for i in range(parts):
-        copies(i)[0].wait()
-        copies(i)[1].start()
-    for i in range(parts):
-        copies(i)[1].wait()
+def fused_kernel(
+    grid, len_ref, enc_ref, w_ref, q_in, g_in,
+    ctx_out, qgrad_out, enc_out, wgrad_out,
+    kv, q, g, ctx, qgrad, prob, grad, kvgrad, local_sem,
+    held, weight, raw, pick, total, raw_sem, send_sem, recv_sem,
+    packed, mix, *rest,
+):
+    R = enc_ref.shape[0]
+
+    def local(src, dst, i):
+        return pltpu.make_async_copy(src, dst, local_sem.at[i])
+
+    local(q_in, q, 0).start()
+    local(g_in, g, 1).start()
+    finish = gather(
+        grid, enc_ref, w_ref, kv, held, weight, raw, pick, total, raw_sem, send_sem, recv_sem
+    )
+    local(q_in, q, 0).wait()
+    local(g_in, g, 1).wait()
+    each(
+        0, grid.S,
+        lambda m: attention_grads(m, R, len_ref, kv, q, g, prob, grad, kvgrad),
+    )
+
+    def while_moving():
+        each(0, grid.S, lambda m: attention_outputs(m, R, kv, prob, grad, ctx, qgrad))
+        local(ctx, ctx_out, 2).start()
+        local(qgrad, qgrad_out, 3).start()
+
+    scatter(grid, kvgrad, enc_out, wgrad_out, while_moving, weight, held, packed, mix, *rest)
+    local(ctx, ctx_out, 2).wait()
+    local(qgrad, qgrad_out, 3).wait()
+    finish()
+
+
+def settle_kernel(count, *refs):
+    sources, targets, buffers = refs[:count], refs[count : 2 * count], refs[2 * count : -2]
+    in_sem, out_sem = refs[-2:]
+    plan = []
+    for source, target, buffer in zip(sources, targets, buffers):
+        parts = 8 if source.shape[0] % 8 == 0 else 1
+        step = source.shape[0] // parts
+        plan += [(source, target, buffer, pl.ds(i * step, step)) for i in range(parts)]
+
+    def load(i):
+        source, _, buffer, rows = plan[i]
+        return pltpu.make_async_copy(source.at[rows], buffer.at[rows], in_sem.at[i])
+
+    def store(i):
+        _, target, buffer, rows = plan[i]
+        return pltpu.make_async_copy(buffer.at[rows], target.at[rows], out_sem.at[i])
+
+    for i in range(len(plan)):
+        load(i).start()
+    for i in range(len(plan)):
+        load(i).wait()
+        store(i).start()
+    for i in range(len(plan)):
+        store(i).wait()
 
 
 def shards(grid, enc_final, enc_len, kv_weight, queries, d_context):
@@ -578,14 +619,27 @@
         kv_weight[0].reshape(D, 2, lane_tiles, LANES).transpose(0, 2, 1, 3)
     ).reshape(D * lane_tiles, 2, LANES)
     sends = Z + (S - 1) * Z + (Y - 1) * Z + 2 * (S - 1) * (Y - 1) * Z + S * Y * Z
-    states, wcat, key_value = pl.pallas_call(
-        functools.partial(gather_kernel, grid),
-        out_shape=(
-            shape((S, M, R, F), bf16), shape((D, 2 * L), bf16), shape((S * R, 2 * L), bf16),
-        ),
-        in_specs=[vmem, anywhere],
-        out_specs=(anywhere, anywhere, vmem),
+    pair = max((S - 1) * (Y - 1) * Z, 1)
+    heads = L // HD
+    results = (
+        shape((S, T, L), bf16), shape((S, T, L), bf16),
+        shape((R, F), bf16), shape((D * lane_tiles, 2, LANES), bf16),
+    )
+    partial = pl.pallas_call(
+        functools.partial(fused_kernel, grid),
+        out_shape=results,
+        in_specs=[pl.BlockSpec(memory_space=pltpu.SMEM), vmem, anywhere, anywhere, anywhere],
+        out_specs=(anywhere, anywhere, vmem, anywhere),
         scratch_shapes=[
+            pltpu.VMEM((S * R, 2 * L), bf16),
+            pltpu.VMEM((S, T, L), bf16),
+            pltpu.VMEM((S, T, L), bf16),
+            pltpu.VMEM((S, T, L), bf16),
+            pltpu.VMEM((S, T, L), bf16),
+            pltpu.VMEM((S, heads * R, T), bf16),
+            pltpu.VMEM((S, heads * R, T), bf16),
+            pltpu.VMEM((S * R, 2 * L), bf16),
+            dma((4,)),
             pltpu.VMEM((S, M, R, F), bf16),
             pltpu.VMEM((D, 2 * L), bf16),
             pltpu.VMEM((D * lane_tiles, 2, LANES), bf16),
@@ -594,37 +648,6 @@
             dma((4,)),
             dma((sends,)),
             dma((2, S, M)),
-            dma((2,)),
-        ],
-        compiler_params=pltpu.CompilerParams(
-            collective_id=0, has_side_effects=True, vmem_limit_bytes=VMEM_BYTES
-        ),
-        name="gather_states",
-    )(enc_final[0], by_lane_tile)
-
-    rows = pl.BlockSpec((R, 2 * L), lambda m: (m, 0))
-    long = pl.BlockSpec((None, T, L), lambda m: (m, 0, 0))
-    context, query_grad, kv_grad = pl.pallas_call(
-        attention_kernel,
-        grid=(S,),
-        out_shape=(
-            shape((S, T, L), bf16), shape((S, T, L), bf16), shape((S * R, 2 * L), bf16),
-        ),
-        in_specs=[pl.BlockSpec(memory_space=pltpu.SMEM), rows, long, long],
-        out_specs=(long, long, rows),
-        compiler_params=pltpu.CompilerParams(vmem_limit_bytes=VMEM_BYTES),
-        name="attention",
-    )(enc_len, key_value, queries[0], d_context[0])
-
-    pair = max((S - 1) * (Y - 1) * Z, 1)
-    enc_grad, weight_grad = pl.pallas_call(
-        functools.partial(scatter_kernel, grid),
-        out_shape=(shape((R, F), bf16), shape((D * lane_tiles, 2, LANES), bf16)),
-        in_specs=[vmem, anywhere, anywhere],
-        out_specs=(vmem, anywhere),
-        scratch_shapes=[
-            pltpu.VMEM((D, 2 * L), bf16),
-            pltpu.VMEM((S, M, R, F), bf16),
             pltpu.VMEM((M, F * lane_tiles, 2, LANES), bf16),
             pltpu.VMEM((2 * LANES, 2 * LANES), bf16),
             pltpu.VMEM((Z * Y, S, R, F), bf16),
@@ -636,7 +659,6 @@
             pltpu.VMEM((max(Y - 1, 1) * Z, R, F), bf16),
             pltpu.VMEM((Z, R, F), bf16),
             pltpu.VMEM((Z, R, F), bf16),
-            dma((2,)),
             dma((Z * Y,)), dma((Z * Y,)),
             dma((pair,)), dma((pair,)), dma((pair,)), dma((pair,)),
             dma((max(S - 1, 1) * Z,)), dma((max(S - 1, 1) * Z,)),
@@ -644,20 +666,24 @@
             dma((Z,)), dma((Z,)), dma((M,)),
         ],
         compiler_params=pltpu.CompilerParams(
-            collective_id=1, has_side_effects=True, vmem_limit_bytes=VMEM_BYTES
+            collective_id=0, has_side_effects=True, vmem_limit_bytes=VMEM_BYTES
         ),
-        name="scatter_states_grad",
-    )(kv_grad, wcat, states)
-
-    weight_grad = pl.pallas_call(
-        settle_kernel,
-        out_shape=shape((D * lane_tiles, 2, LANES), bf16),
-        in_specs=[anywhere],
-        out_specs=anywhere,
-        scratch_shapes=[pltpu.VMEM((D * lane_tiles, 2, LANES), bf16), dma((8,)), dma((8,))],
+        name="cross_attention",
+    )(enc_len, enc_final[0], by_lane_tile, queries[0], d_context[0])
+
+    context, query_grad, enc_grad, weight_grad = pl.pallas_call(
+        functools.partial(settle_kernel, len(results)),
+        out_shape=results,
+        in_specs=[anywhere] * len(results),
+        out_specs=(anywhere,) * len(results),
+        scratch_shapes=[
+            *(pltpu.VMEM(r.shape, r.dtype) for r in results),
+            dma((8 * len(results),)),
+            dma((8 * len(results),)),
+        ],
         compiler_params=pltpu.CompilerParams(vmem_limit_bytes=VMEM_BYTES),
-        name="settle_weight_grad",
-    )(weight_grad)
+        name="settle_results",
+    )(*partial)
     weight_grad = (
         weight_grad.reshape(D, lane_tiles, 2, LANES).transpose(0, 2, 1, 3).reshape(D, 2, L)
     )

time: 57.2 us -> 51.8 us (0.906)
  Pallas kernels: 55.7 us -> 51 us
  local copies, waits for them, and re-layouts: 0.64 us -> 0 us
    pallas_call x4 -> x2, Pallas kernels: 55.7 us -> 51 us  [the longest x1 45.8 us: shards(): pl.pallas_call(functools.partial(fused_kernel, grid), out_shape=results,...]
    unnamed x3 -> x0, local copies, waits for them, and re-layouts: 0.64 us -> none
where the time goes in v4:
time: 51.8 us; the launch traced here: 51.7 us
  Pallas kernels  51 us (98%)
  between operations  0.64 us (1%)
    pallas_call x1, Pallas kernels, shards(): pl.pallas_call(functools.partial(fused_kernel, grid), out_shape=results,...  45.8 us
    pallas_call x1, Pallas kernels, shards(): pl.pallas_call(functools.partial(settle_kernel, len(results)), out_shape=...  5.28 us

profile of v4, /device:TPU:0, one launch (start us, length us, event | category | flops | bytes accessed | tf_op | source)
XLA Modules:
  0.0 51.7 jit_solution(4341949170529448116)
XLA Ops:
  0.6 45.8 %cross_attention.1 = (bf16[2,512,256]{2,1,0:T(8,128)(2,1)}, bf16[2,512,256]{2,1,0:T(8,128)(2,1)}, bf16[128,256]{1,0:T(8,128)(2,1)}, bf16[8192,2,128]{2,1,0:T(2,128)(2,1)}) custom-call(s32[2]{0:T(128)} %len_ref.1, bf16[128,256]{1,0:T(8,128)(2,1)} %bitcast.19, bf16[8192,2,128]{2,1,0:T(2,128)(2,1)} %bitcast.16, bf16[2,512,256]{2,1,0:T(8,128)(2,1)} %bitcast.17, ...), custom_call_target="tpu_custom_call" | custom-call | tf_op jit(solution)/shard_map/cross_attention/pallas_call | solution.py:628
  46.4 5.3 %settle_results.1 = (bf16[2,512,256]{2,1,0:T(8,128)(2,1)}, bf16[2,512,256]{2,1,0:T(8,128)(2,1)}, bf16[128,256]{1,0:T(8,128)(2,1)}, bf16[8192,2,128]{2,1,0:T(2,128)(2,1)}) custom-call(bf16[2,512,256]{2,1,0:T(8,128)(2,1)} %get-tuple-element.12.refs_0_, bf16[2,512,256]{2,1,0:T(8,128)(2,1)} %get-tuple-element.13.refs_1_, ...), custom_call_target="tpu_custom_call" | custom-call | tf_op jit(solution)/shard_map/settle_results/pallas_call | solution.py:674

commit v5 on v4

--- a/solution.py
+++ b/solution.py
@@ -211,9 +211,6 @@
         start(spread(dz))
 
     each(1, Z, column)
-    for i in range(parts // 2, parts):
-        fetch(i).wait()
-    unpack(blocks // 2, blocks)
 
     def multiply(tz, ty, tc):
         p = grid.p(tz, ty, tc)
@@ -231,9 +228,12 @@
         for dy in range(1, Y):
             arrived(grid.tile(x, tz, wrap(y + dy, Y), c))
             start(pass_y(dy, dz))
-        multiply(tz, y, c)
 
     each(0, Z, sides)
+    for i in range(parts // 2, parts):
+        fetch(i).wait()
+    unpack(blocks // 2, blocks)
+    each(0, Z, lambda dz: multiply(wrap(z + dz, Z), y, c))
 
     def diagonal(dz):
         tz = wrap(z + dz, Z)
@@ -583,9 +583,13 @@
     in_sem, out_sem = refs[-2:]
     plan = []
     for source, target, buffer in zip(sources, targets, buffers):
-        parts = 8 if source.shape[0] % 8 == 0 else 1
-        step = source.shape[0] // parts
-        plan += [(source, target, buffer, pl.ds(i * step, step)) for i in range(parts)]
+        axis = 1 if source.shape[0] < 16 else 0
+        parts = 8 if source.shape[axis] % 128 == 0 else 1
+        step = source.shape[axis] // parts
+        for i in range(parts):
+            rows = pl.ds(i * step, step)
+            plan.append((source, target, buffer, (slice(None), rows) if axis else (rows,)))
+    plan.reverse()
 
     def load(i):
         source, _, buffer, rows = plan[i]

time: 51.8 us -> 52.5 us (1.014)
  Pallas kernels: 51 us -> 51.7 us
    pallas_call x1, Pallas kernels: 45.8 us -> 46.7 us  [shards(): pl.pallas_call(functools.partial(fused_kernel, grid), out_shape=results,...]
where the time goes in v5:
time: 52.5 us; the launch traced here: 52.4 us
  Pallas kernels  51.7 us (98%)
  between operations  0.64 us (1%)
    pallas_call x1, Pallas kernels, shards(): pl.pallas_call(functools.partial(fused_kernel, grid), out_shape=results,...  46.7 us
    pallas_call x1, Pallas kernels, shards(): pl.pallas_call(functools.partial(settle_kernel, len(results)), out_shape=...  5.01 us

profile of v5, /device:TPU:0, one launch (start us, length us, event | category | flops | bytes accessed | tf_op | source)
XLA Modules:
  0.0 52.4 jit_solution(10782376940685567487)
XLA Ops:
  0.6 46.7 %cross_attention.1 = (bf16[2,512,256]{2,1,0:T(8,128)(2,1)}, bf16[2,512,256]{2,1,0:T(8,128)(2,1)}, bf16[128,256]{1,0:T(8,128)(2,1)}, bf16[8192,2,128]{2,1,0:T(2,128)(2,1)}) custom-call(s32[2]{0:T(128)} %len_ref.1, bf16[128,256]{1,0:T(8,128)(2,1)} %bitcast.19, bf16[8192,2,128]{2,1,0:T(2,128)(2,1)} %bitcast.16, bf16[2,512,256]{2,1,0:T(8,128)(2,1)} %bitcast.17, ...), custom_call_target="tpu_custom_call" | custom-call | tf_op jit(solution)/shard_map/cross_attention/pallas_call | solution.py:632
  47.4 5.0 %settle_results.1 = (bf16[2,512,256]{2,1,0:T(8,128)(2,1)}, bf16[2,512,256]{2,1,0:T(8,128)(2,1)}, bf16[128,256]{1,0:T(8,128)(2,1)}, bf16[8192,2,128]{2,1,0:T(2,128)(2,1)}) custom-call(bf16[2,512,256]{2,1,0:T(8,128)(2,1)} %get-tuple-element.12.refs_0_, bf16[2,512,256]{2,1,0:T(8,128)(2,1)} %get-tuple-element.13.refs_1_, ...), custom_call_target="tpu_custom_call" | custom-call | tf_op jit(solution)/shard_map/settle_results/pallas_call | solution.py:678
